TPU v7x, 32 devices: a whole 2x2x4 slice. The times are simulated.
32 devices in a mesh: wide: 8 (over z, y), section: 4 (over x, core).
Axes of the slice: x: 2, y: 2, z: 4, core: 2. Of those that a mesh axis runs over, the one named last changes fastest.
Arguments:
- tokens: bfloat16 [64, 200, 768], P('wide'), may hold values from -6 to 6
- cotangent: bfloat16 [64, 200, 768], P('wide'), may hold values from -6 to 6
- patch_grids: int32 [64, 2], P('wide'), may hold values from 8 to 24, as said below
- attention_gain: float32 [2, 768], replicated, may hold values from 0.1 to 1.9
- attention_shift: float32 [2, 768], replicated, may hold values from -3 to 3
- input_projection: bfloat16 [2, 768, 2304], replicated, may hold values from -0.21875 to 0.21875
- query_bias: float32 [2, 768], replicated, may hold values from -3 to 3
- value_bias: float32 [2, 768], replicated, may hold values from -3 to 3
- relative_table: float32 [2, 1269, 12], replicated, may hold values from -4 to 4
- output_projection: bfloat16 [2, 768, 768], replicated, may hold values from -0.875 to 0.875
- output_bias: float32 [2, 768], replicated, may hold values from -2 to 2
- attention_scale: float32 [2, 768], replicated, may hold values from 0.1 to 1.9
- forward_gain: float32 [2, 768], replicated, may hold values from 0.1 to 1.9
- forward_shift: float32 [2, 768], replicated, may hold values from -3 to 3
- hidden_weight: bfloat16 [2, 768, 3072], replicated, may hold values from -0.21875 to 0.21875
- hidden_bias: float32 [2, 3072], replicated, may hold values from -3 to 3
- return_weight: bfloat16 [2, 3072, 768], replicated, may hold values from -0.109375 to 0.109375
- return_bias: float32 [2, 768], replicated, may hold values from -2 to 2
- forward_scale: float32 [2, 768], replicated, may hold values from 0.1 to 1.9
Outputs:
- layer_output: bfloat16 [64, 200, 768], P('wide', None, 'section')
- input_grad: bfloat16 [64, 200, 768], P('wide', None, 'section')
- attention_gain_grad: float32 [2, 768], P(None, 'section')
- attention_shift_grad: float32 [2, 768], P(None, 'section')
- input_projection_grad: float32 [2, 768, 2304], P(None, 'wide', 'section')
- query_bias_grad: float32 [2, 768], P(None, 'section')
- value_bias_grad: float32 [2, 768], P(None, 'section')
- relative_table_grad: float32 [2, 1269, 12], P(None, None, 'section')
- output_projection_grad: float32 [2, 768, 768], P(None, 'wide', 'section')
- output_bias_grad: float32 [2, 768], P(None, 'section')
- attention_scale_grad: float32 [2, 768], P(None, 'section')
- forward_gain_grad: float32 [2, 768], P(None, 'section')
- forward_shift_grad: float32 [2, 768], P(None, 'section')
- hidden_weight_grad: float32 [2, 768, 3072], P(None, 'wide', 'section')
- hidden_bias_grad: float32 [2, 3072], P(None, 'section')
- return_weight_grad: float32 [2, 3072, 768], P(None, 'section', 'wide')
- return_bias_grad: float32 [2, 768], P(None, 'section')
- forward_scale_grad: float32 [2, 768], P(None, 'section')
Inputs may be any that keep to these rules, and one draw needn't show every extreme that they name: `patch_grids`: each row is an image's patch grid (rows, columns): one of (14, 14), (10, 20) and (8, 24); all three occur.
All inputs are finite; a program needn't handle non-finite values.
Results may differ from a plain program's by a relative error of at most 0.018.
Values may be sent and summed in bfloat16 or wider, within the bound.
No kernel may reach another device: no remote copies, remote signals or barrier semaphores. Data moves between devices by JAX's collectives and lax.ppermute only.
A program may use at most 320 MiB of HBM per device.

v0:
```python
import jax
import jax.numpy as jnp
from jax import lax
from jax.sharding import PartitionSpec as P

D = 768
HEADS = 12
HEAD = 64
FF = 3072
ROWS = 200
HMAX = 14
WMAX = 24
REL = 1269
MICRO = 8


def shifted(block, axis, distance):
    devices = range(lax.axis_size(axis))
    route = [(i - distance, i) for i in devices if i - distance in devices]
    return lax.ppermute(block, axis, route)


def as_sent(value):
    return jax.tree.map(lambda a: a.astype(jnp.bfloat16) if a.dtype == jnp.float32 else a, value)


def grid_tables(patch_grids):
    position = jnp.arange(ROWS, dtype=jnp.int32)
    grid_height = patch_grids[..., 0:1]
    grid_width = patch_grids[..., 1:2]
    row_valid = position < grid_height * grid_width
    grid_row = position // grid_width
    grid_column = position % grid_width
    row_gap = jnp.clip(
        grid_row[..., :, None] - grid_row[..., None, :] + (HMAX - 1), 0, 2 * HMAX - 2
    )
    column_gap = jnp.clip(
        grid_column[..., :, None] - grid_column[..., None, :] + (WMAX - 1), 0, 2 * WMAX - 2
    )
    return (row_valid, row_gap * (2 * WMAX - 1) + column_gap)


def norm_forward(values, norm_gain, norm_shift):
    centered = values - jnp.mean(values, axis=-1, keepdims=True)
    inverse = lax.rsqrt(jnp.mean(centered * centered, axis=-1, keepdims=True) + 1e-06)
    whitened = centered * inverse
    return ((whitened * norm_gain + norm_shift).astype(jnp.bfloat16), whitened, inverse)


def norm_backward(upstream, whitened, inverse, norm_gain):
    scaled = upstream * norm_gain
    centered = scaled - jnp.mean(scaled, axis=-1, keepdims=True)
    centered = centered - whitened * jnp.mean(scaled * whitened, axis=-1, keepdims=True)
    return (
        centered * inverse,
        jnp.sum(upstream * whitened, axis=(0, 1)),
        jnp.sum(upstream, axis=(0, 1)),
    )


def dense(inputs, matrix):
    return jnp.einsum("nrd,de->nre", inputs, matrix, preferred_element_type=jnp.float32)


def outer_sum(left, right):
    return jnp.einsum("nrd,nre->de", left, right, preferred_element_type=jnp.float32)


def gelu_slope(hidden):
    return (
        0.5 * (1.0 + lax.erf(hidden * 0.7071067811865476))
        + hidden * jnp.exp(-0.5 * hidden * hidden) * 0.3989422804014327
    )


def attention_inputs(stream, params):
    norm_gain, norm_shift, projection, query_shift, value_shift = params[:5]
    normed, whitened, inverse = norm_forward(stream.astype(jnp.float32), norm_gain, norm_shift)
    projected_all = dense(normed, projection)
    heads_shape = (stream.shape[0], ROWS, HEADS, HEAD)
    queries = (
        ((projected_all[..., :D] + query_shift) * 0.125).astype(jnp.bfloat16).reshape(heads_shape)
    )
    key_heads = projected_all[..., D : 2 * D].astype(jnp.bfloat16).reshape(heads_shape)
    value_heads = (
        (projected_all[..., 2 * D :] + value_shift).astype(jnp.bfloat16).reshape(heads_shape)
    )
    return (normed, whitened, inverse, queries, key_heads, value_heads)


def masked_scores(queries, key_heads, bias_table, row_valid, rel_index):
    scores = jnp.einsum("nihe,njhe->nhij", queries, key_heads, preferred_element_type=jnp.float32)
    scores = scores + jnp.transpose(jnp.take(bias_table, rel_index, axis=0), (0, 3, 1, 2))
    return jnp.where(row_valid[:, None, None, :], scores, -1000000000.0)


def attention_forward(stream, params, row_valid, rel_index):
    normed, whitened, inverse, queries, key_heads, value_heads = attention_inputs(stream, params)
    bias_table, out_matrix, out_shift, layer_scale = params[5:]
    scores = masked_scores(queries, key_heads, bias_table, row_valid, rel_index)
    row_peak = jnp.max(scores, axis=-1, keepdims=True)
    log_total = row_peak + jnp.log(jnp.sum(jnp.exp(scores - row_peak), axis=-1, keepdims=True))
    attention_weights = jnp.exp(scores - log_total).astype(jnp.bfloat16)
    attended = jnp.einsum(
        "nhij,njhe->nihe", attention_weights, value_heads, preferred_element_type=jnp.float32
    )
    attended = attended.reshape(stream.shape[0], ROWS, D).astype(jnp.bfloat16)
    live_rows = row_valid[..., None].astype(jnp.float32)
    branch_out = dense(attended, out_matrix) + out_shift
    return (layer_scale * branch_out * live_rows, log_total[..., 0])


def attention_backward(stream, log_total, upstream, params, row_valid, rel_index):
    normed, whitened, inverse, queries, key_heads, value_heads = attention_inputs(stream, params)
    norm_gain = params[0]
    projection = params[2]
    bias_table, out_matrix, out_shift, layer_scale = params[5:]
    image_count = stream.shape[0]
    heads_shape = (image_count, ROWS, HEADS, HEAD)
    scores = masked_scores(queries, key_heads, bias_table, row_valid, rel_index)
    probability = jnp.exp(scores - log_total[..., None])
    attention_weights = probability.astype(jnp.bfloat16)
    attended = jnp.einsum(
        "nhij,njhe->nihe", attention_weights, value_heads, preferred_element_type=jnp.float32
    )
    attended = attended.reshape(image_count, ROWS, D).astype(jnp.bfloat16)
    live_rows = row_valid[..., None].astype(jnp.float32)
    branch_out = dense(attended, out_matrix) + out_shift
    scale_grad = jnp.sum(upstream * branch_out * live_rows, axis=(0, 1))
    out_rows = (upstream * layer_scale * live_rows).astype(jnp.bfloat16)
    out_shift_grad = jnp.sum(out_rows.astype(jnp.float32), axis=(0, 1))
    attended_grad = jnp.einsum(
        "nre,de->nrd", out_rows, out_matrix, preferred_element_type=jnp.float32
    )
    attended_grad = attended_grad.astype(jnp.bfloat16).reshape(heads_shape)
    weights_grad = jnp.einsum(
        "nihe,njhe->nhij", attended_grad, value_heads, preferred_element_type=jnp.float32
    )
    values_grad = jnp.einsum(
        "nhij,nihe->njhe", attention_weights, attended_grad, preferred_element_type=jnp.float32
    ).astype(jnp.bfloat16)
    score_grad = probability * (
        weights_grad - jnp.sum(weights_grad * probability, axis=-1, keepdims=True)
    )
    score_grad = score_grad.astype(jnp.bfloat16)
    queries_grad = jnp.einsum(
        "nhij,njhe->nihe", score_grad, key_heads, preferred_element_type=jnp.float32
    ).astype(jnp.bfloat16)
    keys_grad = jnp.einsum(
        "nhij,nihe->njhe", score_grad, queries, preferred_element_type=jnp.float32
    ).astype(jnp.bfloat16)
    flat_scores = jnp.transpose(score_grad, (0, 2, 3, 1)).astype(jnp.float32).reshape(-1, HEADS)
    table_grad = jax.ops.segment_sum(flat_scores, rel_index.reshape(-1), num_segments=REL)
    queries_scaled = (
        (queries_grad.astype(jnp.float32) * 0.125)
        .astype(jnp.bfloat16)
        .reshape(image_count, ROWS, D)
    )
    keys_flat = keys_grad.reshape(image_count, ROWS, D)
    values_flat = values_grad.reshape(image_count, ROWS, D)
    projected_grad = jnp.concatenate([queries_scaled, keys_flat, values_flat], axis=-1)
    query_shift_grad = jnp.sum(queries_scaled.astype(jnp.float32), axis=(0, 1))
    value_shift_grad = jnp.sum(values_flat.astype(jnp.float32), axis=(0, 1))
    normed_grad = jnp.einsum(
        "nre,de->nrd", projected_grad, projection, preferred_element_type=jnp.float32
    )
    stream_grad, gain_grad, shift_grad = norm_backward(normed_grad, whitened, inverse, norm_gain)
    smalls = (
        gain_grad,
        shift_grad,
        query_shift_grad,
        value_shift_grad,
        table_grad,
        out_shift_grad,
        scale_grad,
    )
    return (stream_grad, smalls, (normed, projected_grad, attended, out_rows))


def feed_inputs(stream, params):
    norm_gain, norm_shift, hidden_matrix, hidden_shift = params[:4]
    normed, whitened, inverse = norm_forward(stream.astype(jnp.float32), norm_gain, norm_shift)
    hidden = dense(normed, hidden_matrix) + hidden_shift
    return (normed, whitened, inverse, hidden)


def feed_forward(stream, params, row_valid):
    normed, whitened, inverse, hidden = feed_inputs(stream, params)
    return_matrix, return_shift, layer_scale = params[4:]
    active = jax.nn.gelu(hidden, approximate=False).astype(jnp.bfloat16)
    branch_out = dense(active, return_matrix) + return_shift
    return layer_scale * branch_out * row_valid[..., None].astype(jnp.float32)


def feed_backward(stream, upstream, params, row_valid):
    normed, whitened, inverse, hidden = feed_inputs(stream, params)
    norm_gain = params[0]
    hidden_matrix = params[2]
    return_matrix, return_shift, layer_scale = params[4:]
    active = jax.nn.gelu(hidden, approximate=False).astype(jnp.bfloat16)
    live_rows = row_valid[..., None].astype(jnp.float32)
    branch_out = dense(active, return_matrix) + return_shift
    scale_grad = jnp.sum(upstream * branch_out * live_rows, axis=(0, 1))
    out_rows = (upstream * layer_scale * live_rows).astype(jnp.bfloat16)
    return_shift_grad = jnp.sum(out_rows.astype(jnp.float32), axis=(0, 1))
    active_grad = jnp.einsum(
        "nrd,fd->nrf", out_rows, return_matrix, preferred_element_type=jnp.float32
    )
    hidden_grad = (active_grad * gelu_slope(hidden)).astype(jnp.bfloat16)
    hidden_shift_grad = jnp.sum(hidden_grad.astype(jnp.float32), axis=(0, 1))
    normed_grad = jnp.einsum(
        "nrf,df->nrd", hidden_grad, hidden_matrix, preferred_element_type=jnp.float32
    )
    stream_grad, gain_grad, shift_grad = norm_backward(normed_grad, whitened, inverse, norm_gain)
    smalls = (gain_grad, shift_grad, hidden_shift_grad, return_shift_grad, scale_grad)
    return (stream_grad, smalls, (normed, hidden_grad, active, out_rows))


def pick(blocks, micro_slot):
    return lax.dynamic_index_in_dim(blocks, micro_slot, 0, keepdims=False)


def place(blocks, micro_slot, fresh, live_flag):
    merged = jnp.where(live_flag, fresh, pick(blocks, micro_slot))
    return lax.dynamic_update_index_in_dim(blocks, merged, micro_slot, 0)


def store(buffers, fresh, micro_slot):
    return tuple(
        (
            lax.dynamic_update_index_in_dim(buffer, member, micro_slot, 0)
            for buffer, member in zip(buffers, fresh)
        )
    )


def on_device(
    tokens,
    cotangent,
    patch_grids,
    attention_gain,
    attention_shift,
    input_projection,
    query_bias,
    value_bias,
    relative_table,
    output_projection,
    output_bias,
    attention_scale,
    forward_gain,
    forward_shift,
    hidden_weight,
    hidden_bias,
    return_weight,
    return_bias,
    forward_scale,
):
    section_count = lax.axis_size("section")
    layer_count = section_count // 2
    last_section = section_count - 1
    section_index = lax.axis_index("section")
    layer_index = section_index // 2
    half_kind = section_index % 2
    attention_all = (
        attention_gain,
        attention_shift,
        input_projection,
        query_bias,
        value_bias,
        relative_table,
        output_projection,
        output_bias,
        attention_scale,
    )
    feed_all = (
        forward_gain,
        forward_shift,
        hidden_weight,
        hidden_bias,
        return_weight,
        return_bias,
        forward_scale,
    )
    attention_params = tuple(
        (
            lax.dynamic_index_in_dim(member, layer_index, 0, keepdims=False)
            for member in attention_all
        )
    )
    feed_params = tuple(
        (lax.dynamic_index_in_dim(member, layer_index, 0, keepdims=False) for member in feed_all)
    )
    image_count = tokens.shape[0] // MICRO
    token_blocks = tokens.reshape(MICRO, image_count, ROWS, D)
    cot_blocks = cotangent.reshape(MICRO, image_count, ROWS, D)
    valid_all, index_all = grid_tables(patch_grids)
    valid_blocks = valid_all.reshape(MICRO, image_count, ROWS)
    index_blocks = index_all.reshape(MICRO, image_count, ROWS, ROWS)
    ticks_total = MICRO + section_count - 1
    row_shape = (image_count, ROWS, D)

    def forward_tick(clock_tick, state):
        kept_inputs, kept_totals, branch_terms, incoming = state
        micro_index = clock_tick - section_index
        live_flag = (micro_index >= 0) & (micro_index < MICRO)
        micro_slot = jnp.clip(micro_index, 0, MICRO - 1)
        stream = jnp.where(section_index == 0, pick(token_blocks, micro_slot), incoming)
        row_valid = pick(valid_blocks, micro_slot)
        rel_index = pick(index_blocks, micro_slot)

        def forward_spare_case(stream_in):
            return (
                jnp.zeros(row_shape, jnp.float32),
                jnp.zeros((image_count, HEADS, ROWS), jnp.float32),
            )

        def attention_case(stream_in):
            return attention_forward(stream_in, attention_params, row_valid, rel_index)

        def feed_case(stream_in):
            return (
                feed_forward(stream_in, feed_params, row_valid),
                jnp.zeros((image_count, HEADS, ROWS), jnp.float32),
            )

        case_index = jnp.where(live_flag, 1 + half_kind, 0)
        branch, log_total = lax.switch(
            case_index, [forward_spare_case, attention_case, feed_case], stream
        )
        kept_inputs = place(kept_inputs, micro_slot, stream, live_flag)
        kept_totals = place(kept_totals, micro_slot, log_total, live_flag)
        branch_terms = place(branch_terms, micro_slot, branch, live_flag)
        outgoing = jnp.where(live_flag, stream.astype(jnp.float32) + branch, 0.0).astype(
            jnp.bfloat16
        )
        incoming = shifted(outgoing, "section", 1)
        return (kept_inputs, kept_totals, branch_terms, incoming)

    forward_state = (
        jnp.zeros((MICRO,) + row_shape, jnp.bfloat16),
        jnp.zeros((MICRO, image_count, HEADS, ROWS), jnp.float32),
        jnp.zeros((MICRO,) + row_shape, jnp.float32),
        jnp.zeros(row_shape, jnp.bfloat16),
    )
    kept_inputs, kept_totals, branch_terms, incoming = lax.fori_loop(
        0, ticks_total, forward_tick, forward_state
    )
    small_shapes = ((D,), (D,), (D,), (D,), (REL, HEADS), (D,), (D,), (D,), (D,), (FF,), (D,), (D,))
    zero_small = tuple((jnp.zeros(member, jnp.float32) for member in small_shapes))
    zero_grad = jnp.zeros(row_shape, jnp.float32)

    def backward_work(clock_tick, state):
        downstream, input_terms, small_sums, matrix_sums, attention_saved, feed_saved = state
        input_index = clock_tick - (last_section - section_index)
        weight_index = input_index - MICRO
        input_live = (input_index >= 0) & (input_index < MICRO)
        weight_live = (weight_index >= 0) & (weight_index < MICRO)
        input_slot = jnp.clip(input_index, 0, MICRO - 1)
        weight_slot = jnp.clip(weight_index, 0, MICRO - 1)
        stream = pick(kept_inputs, input_slot)
        log_total = pick(kept_totals, input_slot)
        upstream = pick(cot_blocks, input_slot).astype(jnp.float32) + downstream
        row_valid = pick(valid_blocks, input_slot)
        rel_index = pick(index_blocks, input_slot)

        def backward_spare_case(operands):
            return (zero_grad, zero_small, operands[3], operands[4], operands[5])

        def attention_input(operands):
            stream_grad, smalls, saved = attention_backward(
                operands[0], operands[1], operands[2], attention_params, row_valid, rel_index
            )
            return (
                stream_grad,
                smalls + zero_small[7:],
                store(operands[3], saved, input_slot),
                operands[4],
                operands[5],
            )

        def feed_input(operands):
            stream_grad, smalls, saved = feed_backward(
                operands[0], operands[2], feed_params, row_valid
            )
            return (
                stream_grad,
                zero_small[:7] + smalls,
                operands[3],
                store(operands[4], saved, input_slot),
                operands[5],
            )

        def attention_weight(operands):
            normed, projected_grad, attended, out_rows = tuple(
                (pick(buffer, weight_slot) for buffer in operands[3])
            )
            sums = operands[5]
            updated = (
                sums[0] + outer_sum(normed, projected_grad),
                sums[1] + outer_sum(attended, out_rows),
                sums[2],
                sums[3],
            )
            return (zero_grad, zero_small, operands[3], operands[4], updated)

        def feed_weight(operands):
            normed, hidden_grad, active, out_rows = tuple(
                (pick(buffer, weight_slot) for buffer in operands[4])
            )
            sums = operands[5]
            updated = (
                sums[0],
                sums[1],
                sums[2] + outer_sum(normed, hidden_grad),
                sums[3] + outer_sum(active, out_rows),
            )
            return (zero_grad, zero_small, operands[3], operands[4], updated)

        case_index = jnp.where(input_live, 1 + half_kind, jnp.where(weight_live, 3 + half_kind, 0))
        operands = (stream, log_total, upstream, attention_saved, feed_saved, matrix_sums)
        stream_grad, smalls, attention_saved, feed_saved, matrix_sums = lax.switch(
            case_index,
            [backward_spare_case, attention_input, feed_input, attention_weight, feed_weight],
            operands,
        )
        small_sums = tuple((total_part + member for total_part, member in zip(small_sums, smalls)))
        input_terms = place(input_terms, input_slot, stream_grad, input_live)
        outgoing = jnp.where(input_live, downstream + stream_grad, 0.0)
        return (
            (downstream, input_terms, small_sums, matrix_sums, attention_saved, feed_saved),
            outgoing,
        )

    def backward_tick(clock_tick, state):
        fresh, outgoing = backward_work(clock_tick, state)
        downstream = shifted(as_sent(outgoing), "section", -1).astype(outgoing.dtype)
        return (downstream,) + fresh[1:]

    def weight_tick(clock_tick, state):
        fresh, outgoing = backward_work(clock_tick, state)
        return fresh

    matrix_zero = (
        jnp.zeros((D, 3 * D), jnp.float32),
        jnp.zeros((D, D), jnp.float32),
        jnp.zeros((D, FF), jnp.float32),
        jnp.zeros((FF, D), jnp.float32),
    )
    attention_zero = (
        jnp.zeros((MICRO, image_count, ROWS, D), jnp.bfloat16),
        jnp.zeros((MICRO, image_count, ROWS, 3 * D), jnp.bfloat16),
        jnp.zeros((MICRO, image_count, ROWS, D), jnp.bfloat16),
        jnp.zeros((MICRO, image_count, ROWS, D), jnp.bfloat16),
    )
    feed_zero = (
        jnp.zeros((MICRO, image_count, ROWS, D), jnp.bfloat16),
        jnp.zeros((MICRO, image_count, ROWS, FF), jnp.bfloat16),
        jnp.zeros((MICRO, image_count, ROWS, FF), jnp.bfloat16),
        jnp.zeros((MICRO, image_count, ROWS, D), jnp.bfloat16),
    )
    backward_state = (
        zero_grad,
        jnp.zeros((MICRO,) + row_shape, jnp.float32),
        zero_small,
        matrix_zero,
        attention_zero,
        feed_zero,
    )
    backward_state = lax.fori_loop(0, ticks_total, backward_tick, backward_state)
    backward_state = lax.fori_loop(ticks_total, ticks_total + MICRO, weight_tick, backward_state)
    downstream, input_terms, small_sums, matrix_sums, attention_saved, feed_saved = backward_state
    small_sums = lax.psum(
        (
            small_sums[0],
            small_sums[1],
            small_sums[2],
            small_sums[3],
            small_sums[4],
            small_sums[5],
            small_sums[6],
            small_sums[7],
            small_sums[8],
            small_sums[9],
            small_sums[10],
            small_sums[11],
        ),
        "wide",
    )
    projection_sum, out_sum, hidden_sum, return_sum = matrix_sums
    projection_part, out_part, hidden_part, return_part = (
        lax.psum_scatter(projection_sum, "wide", scatter_dimension=0, tiled=True),
        lax.psum_scatter(out_sum, "wide", scatter_dimension=0, tiled=True),
        lax.psum_scatter(hidden_sum, "wide", scatter_dimension=0, tiled=True),
        lax.psum_scatter(return_sum, "wide", scatter_dimension=1, tiled=True),
    )

    def slotted(member):
        return jnp.stack(
            [jnp.where(layer_index == layer_slot, member, 0.0) for layer_slot in range(layer_count)]
        )

    output_terms = branch_terms.reshape(tokens.shape[0], ROWS, D)
    gradient_terms = input_terms.reshape(tokens.shape[0], ROWS, D)
    reduced = (
        lax.psum_scatter(
            output_terms.astype(jnp.bfloat16), "section", scatter_dimension=2, tiled=True
        ).astype(jnp.float32),
        lax.psum_scatter(
            gradient_terms.astype(jnp.bfloat16), "section", scatter_dimension=2, tiled=True
        ).astype(jnp.float32),
        lax.psum_scatter(
            slotted(projection_part).astype(jnp.bfloat16),
            "section",
            scatter_dimension=2,
            tiled=True,
        ).astype(jnp.float32),
        lax.psum_scatter(
            slotted(out_part).astype(jnp.bfloat16), "section", scatter_dimension=2, tiled=True
        ).astype(jnp.float32),
        lax.psum_scatter(
            slotted(hidden_part).astype(jnp.bfloat16), "section", scatter_dimension=2, tiled=True
        ).astype(jnp.float32),
        lax.psum_scatter(
            slotted(return_part).astype(jnp.bfloat16), "section", scatter_dimension=1, tiled=True
        ).astype(jnp.float32),
        lax.psum_scatter(
            slotted(small_sums[0]).astype(jnp.bfloat16), "section", scatter_dimension=1, tiled=True
        ).astype(jnp.float32),
        lax.psum_scatter(
            slotted(small_sums[1]).astype(jnp.bfloat16), "section", scatter_dimension=1, tiled=True
        ).astype(jnp.float32),
        lax.psum_scatter(
            slotted(small_sums[2]).astype(jnp.bfloat16), "section", scatter_dimension=1, tiled=True
        ).astype(jnp.float32),
        lax.psum_scatter(
            slotted(small_sums[3]).astype(jnp.bfloat16), "section", scatter_dimension=1, tiled=True
        ).astype(jnp.float32),
        lax.psum_scatter(
            slotted(small_sums[4]).astype(jnp.bfloat16), "section", scatter_dimension=2, tiled=True
        ).astype(jnp.float32),
        lax.psum_scatter(
            slotted(small_sums[5]).astype(jnp.bfloat16), "section", scatter_dimension=1, tiled=True
        ).astype(jnp.float32),
        lax.psum_scatter(
            slotted(small_sums[6]).astype(jnp.bfloat16), "section", scatter_dimension=1, tiled=True
        ).astype(jnp.float32),
        lax.psum_scatter(
            slotted(small_sums[7]).astype(jnp.bfloat16), "section", scatter_dimension=1, tiled=True
        ).astype(jnp.float32),
        lax.psum_scatter(
            slotted(small_sums[8]).astype(jnp.bfloat16), "section", scatter_dimension=1, tiled=True
        ).astype(jnp.float32),
        lax.psum_scatter(
            slotted(small_sums[9]).astype(jnp.bfloat16), "section", scatter_dimension=1, tiled=True
        ).astype(jnp.float32),
        lax.psum_scatter(
            slotted(small_sums[10]).astype(jnp.bfloat16), "section", scatter_dimension=1, tiled=True
        ).astype(jnp.float32),
        lax.psum_scatter(
            slotted(small_sums[11]).astype(jnp.bfloat16), "section", scatter_dimension=1, tiled=True
        ).astype(jnp.float32),
    )
    feature_width = D // section_count
    token_part = lax.dynamic_slice_in_dim(
        tokens, section_index * feature_width, feature_width, 2
    ).astype(jnp.float32)
    cot_part = lax.dynamic_slice_in_dim(
        cotangent, section_index * feature_width, feature_width, 2
    ).astype(jnp.float32)
    layer_output = (token_part + reduced[0]).astype(jnp.bfloat16)
    input_grad = (cot_part + reduced[1]).astype(jnp.bfloat16)
    return (
        layer_output,
        input_grad,
        reduced[6],
        reduced[7],
        reduced[2],
        reduced[8],
        reduced[9],
        reduced[10],
        reduced[3],
        reduced[11],
        reduced[12],
        reduced[13],
        reduced[14],
        reduced[4],
        reduced[15],
        reduced[5],
        reduced[16],
        reduced[17],
    )


def solution(mesh):
    return jax.shard_map(
        on_device,
        mesh=mesh,
        in_specs=(
            P("wide", None, None),
            P("wide", None, None),
            P("wide", None),
            P(),
            P(),
            P(),
            P(),
            P(),
            P(),
            P(),
            P(),
            P(),
            P(),
            P(),
            P(),
            P(),
            P(),
            P(),
            P(),
        ),
        out_specs=(
            P("wide", None, "section"),
            P("wide", None, "section"),
            P(None, "section"),
            P(None, "section"),
            P(None, "wide", "section"),
            P(None, "section"),
            P(None, "section"),
            P(None, None, "section"),
            P(None, "wide", "section"),
            P(None, "section"),
            P(None, "section"),
            P(None, "section"),
            P(None, "section"),
            P(None, "wide", "section"),
            P(None, "section"),
            P(None, "section", "wide"),
            P(None, "section"),
            P(None, "section"),
        ),
        check_vma=False,
    )
```

profile of v0, /device:TPU:0, one launch (start us, length us, event | category | flops | bytes accessed | tf_op | source)
XLA Modules:
  0.0 6005.2 jit_solution(12046470802829316848)
XLA Ops:
  33.4 1124.5 %while.152 = (s32[]{:T(128)}, bf16[8,1,200,768]{3,2,1,0:T(8,128)(2,1)}, f32[8,1,12,200]{3,2,1,0:T(8,128)}, bf16[8,1,200,768]{3,2,1,0:T(8,128)(2,1)}, bf16[1,200,...) while((s32[]{:T(128)}, ...), condition=%wide.region_10.12_spmd.clone, body=%wide.region_0.11_spmd.clone.sunk | while | flops 1931369216 | bytes 43370092 | solution.py:345
  1041.2 113.0 %collective-permute-start = (bf16[1,200,768]{2,1,0:T(8,128)(2,1)S(1)}, bf16[1,200,768]{2,1,0:T(8,128)(2,1)}, u32[]{:S(2)}, u32[]{:S(2)}) collective-permute-start(bf16[1,200,768]{2,1,0:T(8,128)(2,1)S(1)} %select_convert_fusion.36), channel_id=1, source_target_pairs={{0,1},{1,2},{2,3},{4,5},{5,6},{6,7},{8,9},{9,10},{10,11},{12,13},{... | collective-permute-start | bytes 921608 | tf_op jit(solution)/shard_map/while/body/eval_jaxpr/ppermute | solution.py:20
  1195.6 3510.4 %while.154 = (s32[]{:T(128)}, f32[1,200,768]{2,1,0:T(8,128)S(1)}, bf16[8,1,200,768]{3,2,1,0:T(8,128)(2,1)}, f32[768]{0:T(1024)}, f32[768]{0:T(1024)}, /*index=5*...) while((s32[]{:T(128)}, f32[1,200,768]{2,1,0:T(8,128)S(1)}, ...), condition=%wide.region_39.41_spmd.clone, body=%wide.region_12.40_spmd.clone.sunk | while | flops 3831291136 | bytes 129140064 | solution.py:469
  1258.8 386.4 %collective-permute-done.1 = bf16[1,200,768]{2,1,0:T(8,128)(2,1)S(1)} collective-permute-done((bf16[1,200,768]{2,1,0:T(8,128)(2,1)S(1)}, bf16[1,200,768]{2,1,0:T(8,128)(2,1)S(1)}, u32[]{:S(2)}, u32[]{:S(2)}) %collective-permute-start.1) | collective-permute-done | bytes 307232 | tf_op jit(solution)/shard_map/while/body/eval_jaxpr/ppermute | solution.py:20
  1649.6 365.2 %conditional.11 = (f32[1,200,768]{2,1,0:T(8,128)S(1)}, f32[768]{0:T(1024)}, f32[768]{0:T(1024)}, f32[768]{0:T(1024)}, f32[768]{0:T(1024)}, /*index=5*/f32[1269,1...) conditional(s32[]{:T(128)} %clamp.59, ...), branch_computations={%region_13.14_spmd, %region_14.27_spmd.clone, %region_27.37_spmd, ... | conditional | flops 3829856768 | bytes 117038912 | solution.py:421
  1790.0 216.6 %scatter_custom_fusion.3 = f32[1269,12]{1,0:T(8,128)} fusion(s32[40000]{0:T(1024)S(1)} %reshape.1743, f32[40000,12]{1,0:T(8,128)} %bitcast.663, f32[]{:T(128)} %constant.693.clone.1), kind=kCustom, calls=%fused_computation.459 | custom fusion | flops 480000 | bytes 61424 | tf_op jit(solution)/shard_map/while/body/eval_jaxpr/cond/branch_1_fun/scatter-add | solution.py:153
  2030.1 365.2 %conditional.11 = (f32[1,200,768]{2,1,0:T(8,128)S(1)}, f32[768]{0:T(1024)}, f32[768]{0:T(1024)}, f32[768]{0:T(1024)}, f32[768]{0:T(1024)}, /*index=5*/f32[1269,1...) conditional(s32[]{:T(128)} %clamp.59, ...), branch_computations={%region_13.14_spmd, %region_14.27_spmd.clone, %region_27.37_spmd, ... | conditional | flops 3829856768 | bytes 117038912 | solution.py:421
  2170.5 216.6 %scatter_custom_fusion.3 = f32[1269,12]{1,0:T(8,128)} fusion(s32[40000]{0:T(1024)S(1)} %reshape.1743, f32[40000,12]{1,0:T(8,128)} %bitcast.663, f32[]{:T(128)} %constant.693.clone.1), kind=kCustom, calls=%fused_computation.459 | custom fusion | flops 480000 | bytes 61424 | tf_op jit(solution)/shard_map/while/body/eval_jaxpr/cond/branch_1_fun/scatter-add | solution.py:153
  2410.2 365.2 %conditional.11 = (f32[1,200,768]{2,1,0:T(8,128)S(1)}, f32[768]{0:T(1024)}, f32[768]{0:T(1024)}, f32[768]{0:T(1024)}, f32[768]{0:T(1024)}, /*index=5*/f32[1269,1...) conditional(s32[]{:T(128)} %clamp.59, ...), branch_computations={%region_13.14_spmd, %region_14.27_spmd.clone, %region_27.37_spmd, ... | conditional | flops 3829856768 | bytes 117038912 | solution.py:421
  2550.6 216.6 %scatter_custom_fusion.3 = f32[1269,12]{1,0:T(8,128)} fusion(s32[40000]{0:T(1024)S(1)} %reshape.1743, f32[40000,12]{1,0:T(8,128)} %bitcast.663, f32[]{:T(128)} %constant.693.clone.1), kind=kCustom, calls=%fused_computation.459 | custom fusion | flops 480000 | bytes 61424 | tf_op jit(solution)/shard_map/while/body/eval_jaxpr/cond/branch_1_fun/scatter-add | solution.py:153
  2790.9 365.2 %conditional.11 = (f32[1,200,768]{2,1,0:T(8,128)S(1)}, f32[768]{0:T(1024)}, f32[768]{0:T(1024)}, f32[768]{0:T(1024)}, f32[768]{0:T(1024)}, /*index=5*/f32[1269,1...) conditional(s32[]{:T(128)} %clamp.59, ...), branch_computations={%region_13.14_spmd, %region_14.27_spmd.clone, %region_27.37_spmd, ... | conditional | flops 3829856768 | bytes 117038912 | solution.py:421
  2931.3 216.6 %scatter_custom_fusion.3 = f32[1269,12]{1,0:T(8,128)} fusion(s32[40000]{0:T(1024)S(1)} %reshape.1743, f32[40000,12]{1,0:T(8,128)} %bitcast.663, f32[]{:T(128)} %constant.693.clone.1), kind=kCustom, calls=%fused_computation.459 | custom fusion | flops 480000 | bytes 61424 | tf_op jit(solution)/shard_map/while/body/eval_jaxpr/cond/branch_1_fun/scatter-add | solution.py:153
  3171.1 365.2 %conditional.11 = (f32[1,200,768]{2,1,0:T(8,128)S(1)}, f32[768]{0:T(1024)}, f32[768]{0:T(1024)}, f32[768]{0:T(1024)}, f32[768]{0:T(1024)}, /*index=5*/f32[1269,1...) conditional(s32[]{:T(128)} %clamp.59, ...), branch_computations={%region_13.14_spmd, %region_14.27_spmd.clone, %region_27.37_spmd, ... | conditional | flops 3829856768 | bytes 117038912 | solution.py:421
  3311.6 216.6 %scatter_custom_fusion.3 = f32[1269,12]{1,0:T(8,128)} fusion(s32[40000]{0:T(1024)S(1)} %reshape.1743, f32[40000,12]{1,0:T(8,128)} %bitcast.663, f32[]{:T(128)} %constant.693.clone.1), kind=kCustom, calls=%fused_computation.459 | custom fusion | flops 480000 | bytes 61424 | tf_op jit(solution)/shard_map/while/body/eval_jaxpr/cond/branch_1_fun/scatter-add | solution.py:153
  3551.6 365.2 %conditional.11 = (f32[1,200,768]{2,1,0:T(8,128)S(1)}, f32[768]{0:T(1024)}, f32[768]{0:T(1024)}, f32[768]{0:T(1024)}, f32[768]{0:T(1024)}, /*index=5*/f32[1269,1...) conditional(s32[]{:T(128)} %clamp.59, ...), branch_computations={%region_13.14_spmd, %region_14.27_spmd.clone, %region_27.37_spmd, ... | conditional | flops 3829856768 | bytes 117038912 | solution.py:421
  3692.0 216.6 %scatter_custom_fusion.3 = f32[1269,12]{1,0:T(8,128)} fusion(s32[40000]{0:T(1024)S(1)} %reshape.1743, f32[40000,12]{1,0:T(8,128)} %bitcast.663, f32[]{:T(128)} %constant.693.clone.1), kind=kCustom, calls=%fused_computation.459 | custom fusion | flops 480000 | bytes 61424 | tf_op jit(solution)/shard_map/while/body/eval_jaxpr/cond/branch_1_fun/scatter-add | solution.py:153
  3932.0 365.2 %conditional.11 = (f32[1,200,768]{2,1,0:T(8,128)S(1)}, f32[768]{0:T(1024)}, f32[768]{0:T(1024)}, f32[768]{0:T(1024)}, f32[768]{0:T(1024)}, /*index=5*/f32[1269,1...) conditional(s32[]{:T(128)} %clamp.59, ...), branch_computations={%region_13.14_spmd, %region_14.27_spmd.clone, %region_27.37_spmd, ... | conditional | flops 3829856768 | bytes 117038912 | solution.py:421
  4072.4 216.6 %scatter_custom_fusion.3 = f32[1269,12]{1,0:T(8,128)} fusion(s32[40000]{0:T(1024)S(1)} %reshape.1743, f32[40000,12]{1,0:T(8,128)} %bitcast.663, f32[]{:T(128)} %constant.693.clone.1), kind=kCustom, calls=%fused_computation.459 | custom fusion | flops 480000 | bytes 61424 | tf_op jit(solution)/shard_map/while/body/eval_jaxpr/cond/branch_1_fun/scatter-add | solution.py:153
  4312.2 365.1 %conditional.11 = (f32[1,200,768]{2,1,0:T(8,128)S(1)}, f32[768]{0:T(1024)}, f32[768]{0:T(1024)}, f32[768]{0:T(1024)}, f32[768]{0:T(1024)}, /*index=5*/f32[1269,1...) conditional(s32[]{:T(128)} %clamp.59, ...), branch_computations={%region_13.14_spmd, %region_14.27_spmd.clone, %region_27.37_spmd, ... | conditional | flops 3829856768 | bytes 117038912 | solution.py:421
  4452.5 216.6 %scatter_custom_fusion.3 = f32[1269,12]{1,0:T(8,128)} fusion(s32[40000]{0:T(1024)S(1)} %reshape.1743, f32[40000,12]{1,0:T(8,128)} %bitcast.663, f32[]{:T(128)} %constant.693.clone.1), kind=kCustom, calls=%fused_computation.459 | custom fusion | flops 480000 | bytes 61424 | tf_op jit(solution)/shard_map/while/body/eval_jaxpr/cond/branch_1_fun/scatter-add | solution.py:153
  4705.9 305.1 %while.153 = (s32[]{:T(128)}, bf16[8,1,200,768]{3,2,1,0:T(8,128)(2,1)}, f32[768]{0:T(1024)}, f32[768]{0:T(1024)}, f32[768]{0:T(1024)}, /*index=5*/f32[768]{0:T(1...) while((s32[]{:T(128)}, ...), condition=%wide.region_67.69_spmd.clone, body=%wide.region_40.68_spmd.clone.sunk | while | flops 3830497024 | bytes 127198312 | solution.py:470
  5093.7 129.3 %reduce-scatter.52.cloned.1.call-done = f32[96,2304]{1,0:T(8,128)} async-done(((f32[768,2304]{1,0:T(8,128)}), f32[96,2304]{1,0:T(8,128)}) %reduce-scatter.52.cloned.1.call-update) | async-done | bytes 884752 | tf_op jit(solution)/shard_map/reduce_scatter | solution.py:491
  5227.8 161.8 %reduce-scatter.56.cloned.1.call-done = f32[96,3072]{1,0:T(8,128)} async-done(((f32[768,3072]{1,0:T(8,128)}), f32[96,3072]{1,0:T(8,128)}) %reduce-scatter.56.cloned.1.call-update) | async-done | bytes 1179664 | tf_op jit(solution)/shard_map/reduce_scatter | solution.py:493
  5392.2 163.9 %reduce-scatter.60.cloned.1.call-done = f32[3072,96]{0,1:T(8,128)} async-done(((f32[3072,768]{0,1:T(8,128)}), f32[3072,96]{0,1:T(8,128)}) %reduce-scatter.60.cloned.1.call-update) | async-done | bytes 1179664 | tf_op jit(solution)/shard_map/reduce_scatter | solution.py:494
  (2849 shorter events, 4305.7 us)
Async XLA Ops:
  7.2 5084.0 %reduce-scatter.54.cloned.1.call-start = ((), (), s32[]{:S(2)}) async-start(), calls=%async_computation.24 | async-start | bytes 2654208 | tf_op jit(solution)/shard_map/reduce_scatter | solution.py:492
  1012.1 23.6 collective-permute-start
  1041.2 116.1 %collective-permute-start = (bf16[1,200,768]{2,1,0:T(8,128)(2,1)S(1)}, bf16[1,200,768]{2,1,0:T(8,128)(2,1)}, u32[]{:S(2)}, u32[]{:S(2)}) collective-permute-start(bf16[1,200,768]{2,1,0:T(8,128)(2,1)S(1)} %select_convert_fusion.36), channel_id=1, source_target_pairs={{0,1},{1,2},{2,3},{4,5},{5,6},{6,7},{8,9},{9,10},{10,11},{12,13},{... | collective-permute-start | bytes 921608 | tf_op jit(solution)/shard_map/while/body/eval_jaxpr/ppermute | solution.py:20
  1249.9 395.3 %collective-permute-start.1 = (bf16[1,200,768]{2,1,0:T(8,128)(2,1)S(1)}, bf16[1,200,768]{2,1,0:T(8,128)(2,1)S(1)}, u32[]{:S(2)}, u32[]{:S(2)}) collective-permute-start(bf16[1,200,768]{2,1,0:T(8,128)(2,1)S(1)} %select_convert_fusion.37), channel_id=1, source_target_pairs={{1,0},{2,1},{3,2},{5,4},{6,5},{7,6},{9,8},{10,9},{11,10},{13,12},{... | collective-permute-start | bytes 921608 | tf_op jit(solution)/shard_map/while/body/eval_jaxpr/ppermute | solution.py:20
  5011.1 211.9 %reduce-scatter.52.cloned.1.call-start = ((), (), s32[]{:S(2)}) async-start(), calls=%async_computation.23 | async-start | bytes 7962624 | tf_op jit(solution)/shard_map/reduce_scatter | solution.py:491
  5011.8 377.7 %reduce-scatter.56.cloned.1.call-start = ((), (), s32[]{:S(2)}) async-start(), calls=%async_computation.25 | async-start | bytes 10616832 | tf_op jit(solution)/shard_map/reduce_scatter | solution.py:493
  5012.6 543.5 %reduce-scatter.60.cloned.1.call-start = ((), (), s32[]{:S(2)}) async-start(), calls=%async_computation.27 | async-start | bytes 10616832 | tf_op jit(solution)/shard_map/reduce_scatter | solution.py:494
  5022.4 555.5 %reduce-scatter.64.cloned.1.call-start = ((), (), s32[]{:S(2)}) async-start(), calls=%async_computation.29 | async-start | bytes 245760
  5066.1 534.6 %reduce-scatter.66.cloned.1.call-start = ((), (), s32[]{:S(2)}) async-start(), calls=%async_computation.30 | async-start | bytes 245760
  5067.1 556.5 %reduce-scatter.70.cloned.1.call-start = ((), (), s32[]{:S(2)}) async-start(), calls=%async_computation.32 | async-start | bytes 245760
  5068.1 578.5 %reduce-scatter.72.cloned.1.call-start = ((), (), s32[]{:S(2)}) async-start(), calls=%async_computation.33 | async-start | bytes 245760
  5069.1 599.8 %reduce-scatter.76.cloned.1.call-start = ((), (), s32[]{:S(2)}) async-start(), calls=%async_computation.35 | async-start | bytes 245760
  5070.0 621.1 %reduce-scatter.78.cloned.1.call-start = ((), (), s32[]{:S(2)}) async-start(), calls=%async_computation.36 | async-start | bytes 245760
  5071.0 642.4 %reduce-scatter.80.cloned.1.call-start = ((), (), s32[]{:S(2)}) async-start(), calls=%async_computation.37 | async-start | bytes 245760
  5072.0 663.7 %reduce-scatter.82.cloned.1.call-start = ((), (), s32[]{:S(2)}) async-start(), calls=%async_computation.38 | async-start | bytes 245760
  5073.0 685.0 %reduce-scatter.86.cloned.1.call-start = ((), (), s32[]{:S(2)}) async-start(), calls=%async_computation.40 | async-start | bytes 245760
  5074.0 706.3 %reduce-scatter.88.cloned.1.call-start = ((), (), s32[]{:S(2)}) async-start(), calls=%async_computation.41 | async-start | bytes 245760
  5074.9 731.7 %reduce-scatter.84.cloned.1.call-start = ((), (), s32[]{:S(2)}) async-start(), calls=%async_computation.39 | async-start | bytes 983040
  5076.3 770.7 %reduce-scatter.48.cloned.1.call-start = ((), (), s32[]{:S(2)}) async-start(), calls=%async_computation.21 | async-start | bytes 3932160 | tf_op jit(solution)/shard_map/reduce_scatter | solution.py:505
  5080.9 806.7 %reduce-scatter.50.cloned.1.call-start = ((), (), s32[]{:S(2)}) async-start(), calls=%async_computation.22 | async-start | bytes 3932160 | tf_op jit(solution)/shard_map/reduce_scatter | solution.py:508
  5085.5 825.8 %reduce-scatter.74.cloned.1.call-start = ((), (), s32[]{:S(2)}) async-start(), calls=%async_computation.34 | async-start | bytes 491520
  5093.6 846.1 %reduce-scatter.68.cloned.1.call-start = ((), (), s32[]{:S(2)}) async-start(), calls=%async_computation.31 | async-start | bytes 1474560
  5227.7 740.3 %reduce-scatter.58.cloned.1.call-start = ((), (), s32[]{:S(2)}) async-start(), calls=%async_computation.26 | async-start | bytes 1474560 | tf_op jit(solution)/shard_map/reduce_scatter | solution.py:520
  5392.1 604.2 %reduce-scatter.62.cloned.1.call-start = ((), (), s32[]{:S(2)}) async-start(), calls=%async_computation.28 | async-start | bytes 1474560 | tf_op jit(solution)/shard_map/reduce_scatter | solution.py:523
  (694 other events, 17741.9 us)
Sparse Core Ops, SparseCore 0:
  5011.2 79.9 reduce-scatter.53
  5094.8 128.0 reduce-scatter.51
  5227.0 162.5 reduce-scatter.55
  5393.4 162.5 reduce-scatter.59
  5559.0 18.8 reduce-scatter.63
  5580.9 19.7 reduce-scatter.65
  5603.8 19.7 reduce-scatter.69
  5626.8 19.7 reduce-scatter.71
  5649.1 19.7 reduce-scatter.75
  5671.3 19.7 reduce-scatter.77
  5693.7 19.7 reduce-scatter.79
  5715.9 19.7 reduce-scatter.81
  5738.2 19.7 reduce-scatter.85
  5760.5 19.7 reduce-scatter.87
  5783.3 23.2 reduce-scatter.83
  5809.0 37.9 reduce-scatter.47
  5849.6 37.9 reduce-scatter.49
  5890.5 20.8 reduce-scatter.73
  5913.9 25.7 reduce-scatter.67
  5942.3 25.7 reduce-scatter.57
  5970.6 25.7 reduce-scatter.61
where the time goes:
time: 6030 us; the launch traced here: 6010 us
  other arithmetic  2130 us (35%)
  local copies, waits for them, and re-layouts  2030 us (34%)
  waiting for transfers between devices  1250 us (21%)
  matrix products  311 us (5%)
  starting transfers between devices  176 us (3%)
    scatter-add x8, other arithmetic, attention_backward(): jax.ops.segment_sum(flat_scores, rel_index.reshape(-1), num_segments=REL)  1730 us
    gather x32, local copies, waits for them, and re-layouts, masked_scores(): jnp.take(bias_table, rel_index, axis=0)  1410 us
    ppermute x22, waiting for transfers between devices, shifted(): return lax.ppermute(block, axis, route)  391 us
    unnamed x34, waiting for transfers between devices  265 us
    ppermute x22, starting transfers between devices, shifted(): return lax.ppermute(block, axis, route)  175 us
    reduce_scatter x1, waiting for transfers between devices, on_device(): lax.psum_scatter(return_sum, 'wide', scatter_dimension=1, tiled=True)  164 us
    reduce_scatter x1, waiting for transfers between devices, on_device(): lax.psum_scatter(hidden_sum, 'wide', scatter_dimension=0, tiled=True)  162 us
    add x173, other arithmetic, backward_work(): total_part + member  158 us
  transfers between devices with their start and end apart: 43, of which 30 were waited for; matrix products, arithmetic and copies ran while one was open for 3% of the time, Pallas kernels for 0%

commit v1 on v0

v1 whole, which is shorter than its diff:
```python
import functools

import jax
import jax.numpy as jnp
from jax import lax
from jax.experimental import pallas as pl
from jax.experimental.pallas import tpu as pltpu
from jax.sharding import PartitionSpec as P

D = 768
HEADS = 12
HEAD = 64
FF = 3072
ROWS = 200
HMAX = 14
WMAX = 24
REL = 1269
LAYERS = 2
QW = 2 * WMAX - 1
PITCH = 64
RP = 208
ROWK = HMAX * WMAX
COLK = HMAX * PITCH
TABW = 2 * HMAX * PITCH
QUAD = 4
F32 = jnp.float32
BF16 = jnp.bfloat16
NN = (((1,), (0,)), ((), ()))
NT = (((1,), (1,)), ((), ()))
TN = (((0,), (0,)), ((), ()))
VMEM = 52 * 1024 * 1024


def dot(left, right, dims=NN):
    return lax.dot_general(left, right, dims, preferred_element_type=F32)


def params(**more):
    return pltpu.CompilerParams(vmem_limit_bytes=VMEM, **more)


def whole(*shape):
    return pl.BlockSpec(shape, lambda *_: (0,) * len(shape))


def norm_stats(u):
    mean = jnp.mean(u, axis=1, keepdims=True)
    centered = u - mean
    inverse = lax.rsqrt(jnp.mean(centered * centered, axis=1, keepdims=True) + 1e-6)
    return centered * inverse, inverse


def norm_back(upstream, whitened, inverse, gain):
    scaled = upstream * gain
    first = jnp.mean(scaled, axis=1, keepdims=True)
    second = jnp.mean(scaled * whitened, axis=1, keepdims=True)
    return (scaled - first - whitened * second) * inverse


def column_sum(v):
    return jnp.sum(v, axis=0, keepdims=True)


def head_masks():
    lane = lax.broadcasted_iota(jnp.int32, (1, 2 * HEAD), 1)
    low = (lane < HEAD).astype(F32)
    return low.astype(BF16), (1.0 - low).astype(BF16)


def skewed(row):
    return pltpu.roll(jnp.broadcast_to(row, (WMAX, TABW)), 0, 1, stride=1, stride_axis=0)


def attention_forward_kernel(
    images, u_ref, total_ref, gain_ref, shift_ref, wq_ref, wk_ref, wv_ref, qb_ref, vb_ref, table_ref,
    wo_ref, ob_ref, scale_ref, live_ref, mask_ref, s_ref, pt_ref,
    next_ref, newtotal_ref, normed_ref, q_ref, k_ref, v_ref, att_ref, w_ref, branch_ref,
    acc_ref, rst_ref,
):
    step = pl.program_id(0)

    @pl.when(step == 0)
    def _():
        whitened, _ = norm_stats(u_ref[...].astype(F32))
        normed_ref[...] = (whitened * gain_ref[...] + shift_ref[...]).astype(BF16)
        acc_ref[...] = jnp.zeros_like(acc_ref)

    normed = normed_ref[...]
    q_ref[...] = ((dot(normed, wq_ref[...]) + qb_ref[...]) * 0.125).astype(BF16)
    k_ref[...] = dot(normed, wk_ref[...]).astype(BF16)
    v_ref[...] = (dot(normed, wv_ref[...]) + vb_ref[...]).astype(BF16)
    masks = head_masks()
    for pair in range(QUAD // 2):
        lanes = slice(128 * pair, 128 * pair + 128)
        for e in range(2):
            base = skewed(table_ref[2 * pair + e])
            odd = pltpu.roll(base, TABW - PITCH, 1)
            for a in range(0, HMAX, 2):
                both = jnp.concatenate(
                    [base[:, PITCH * a : PITCH * a + COLK], odd[:, PITCH * a : PITCH * a + COLK]], axis=0
                )
                at = ROWK * e + WMAX * a
                rst_ref[at : at + 2 * WMAX, :] = both.astype(BF16)
        for n in range(images):
            rows = slice(RP * n, RP * n + RP)
            spread = dot(rst_ref[...], s_ref[n]).astype(BF16)
            qn, kn, vn = q_ref[rows, lanes], k_ref[rows, lanes], v_ref[rows, lanes]
            attended = None
            for e in range(2):
                bias = dot(pt_ref[n], spread[ROWK * e : ROWK * e + ROWK])
                scores = dot(qn * masks[e], kn, NT) + (bias + mask_ref[n])
                peak = jnp.max(scores, axis=1, keepdims=True)
                power = jnp.exp(scores - peak)
                weights = (power * (1.0 / jnp.sum(power, axis=1, keepdims=True))).astype(BF16)
                w_ref[n, 2 * pair + e] = weights
                part = dot(weights, vn * masks[e])
                attended = part if attended is None else attended + part
            att_ref[rows, lanes] = attended.astype(BF16)
    acc_ref[...] += dot(att_ref[...], wo_ref[...])

    @pl.when(step == pl.num_programs(0) - 1)
    def _():
        out = acc_ref[...] + ob_ref[...]
        branch_ref[...] = out.astype(BF16)
        branch = scale_ref[...] * out * live_ref[...]
        next_ref[...] = (u_ref[...].astype(F32) + branch).astype(BF16)
        newtotal_ref[...] = total_ref[...] + branch


def row_of(layer, width=D):
    return pl.BlockSpec((None, 1, width), lambda *_: (layer, 0, 0))


def attention_forward(layer, images, u, total, w, tables):
    m = u.shape[0]
    live, mask, s, pt = tables["live"], tables["mask"], tables["s"], tables["pt"]
    wide = QUAD * HEAD
    steps = HEADS // QUAD
    third = lambda which: pl.BlockSpec((None, D, wide), lambda g: (layer, 0, which * steps + g))
    block = pl.BlockSpec((m, wide), lambda g: (0, g))
    out_type = [
        jax.ShapeDtypeStruct((m, D), BF16),
        jax.ShapeDtypeStruct((m, D), F32),
        jax.ShapeDtypeStruct((m, D), BF16),
        jax.ShapeDtypeStruct((m, D), BF16),
        jax.ShapeDtypeStruct((m, D), BF16),
        jax.ShapeDtypeStruct((m, D), BF16),
        jax.ShapeDtypeStruct((m, D), BF16),
        jax.ShapeDtypeStruct((images, HEADS, RP, RP), BF16),
        jax.ShapeDtypeStruct((m, D), BF16),
    ]
    return pl.pallas_call(
        functools.partial(attention_forward_kernel, images),
        grid=(steps,),
        in_specs=[
            whole(m, D), whole(m, D), row_of(layer), row_of(layer), third(0), third(1), third(2),
            pl.BlockSpec((None, 1, wide), lambda g: (layer, 0, g)),
            pl.BlockSpec((None, 1, wide), lambda g: (layer, 0, g)),
            pl.BlockSpec((None, QUAD, 1, TABW), lambda g: (layer, g, 0, 0)),
            pl.BlockSpec((None, wide, D), lambda g: (layer, g, 0)),
            row_of(layer), row_of(layer), whole(m, 1), whole(images, 1, RP),
            whole(images, COLK, RP), whole(images, RP, ROWK),
        ],
        out_specs=[
            whole(m, D), whole(m, D), whole(m, D), block, block, block, block,
            pl.BlockSpec((images, QUAD, RP, RP), lambda g: (0, g, 0, 0)),
            whole(m, D),
        ],
        out_shape=out_type,
        scratch_shapes=[pltpu.VMEM((m, D), F32), pltpu.VMEM((2 * ROWK, COLK), BF16)],
        compiler_params=params(),
        cost_estimate=pl.CostEstimate(flops=12 * 10**9, bytes_accessed=15 * 10**6, transcendentals=10**6),
        name="attention_forward",
    )(
        u, total, w["attention_gain"], w["attention_shift"], w["input_projection"], w["input_projection"],
        w["input_projection"], w["query_bias"], w["value_bias"], tables["table"], w["output_projection"],
        w["output_bias"], w["attention_scale"], live, mask, s, pt,
    )


def feed_forward_kernel(
    u_ref, total_ref, gain_ref, shift_ref, wh_ref, hb_ref, wr_ref, rb_ref, scale_ref, live_ref,
    next_ref, newtotal_ref, normed_ref, active_ref, slope_ref, branch_ref, acc_ref,
):
    step = pl.program_id(0)

    @pl.when(step == 0)
    def _():
        whitened, _ = norm_stats(u_ref[...].astype(F32))
        normed_ref[...] = (whitened * gain_ref[...] + shift_ref[...]).astype(BF16)
        acc_ref[...] = jnp.zeros_like(acc_ref)

    hidden = dot(normed_ref[...], wh_ref[...]) + hb_ref[...]
    share = 0.5 * (1.0 + lax.erf(hidden * 0.7071067811865476))
    active_ref[...] = (hidden * share).astype(BF16)
    slope_ref[...] = (share + hidden * jnp.exp(-0.5 * hidden * hidden) * 0.3989422804014327).astype(BF16)
    acc_ref[...] += dot(active_ref[...], wr_ref[...])

    @pl.when(step == pl.num_programs(0) - 1)
    def _():
        out = acc_ref[...] + rb_ref[...]
        branch_ref[...] = out.astype(BF16)
        branch = scale_ref[...] * out * live_ref[...]
        next_ref[...] = (u_ref[...].astype(F32) + branch).astype(BF16)
        newtotal_ref[...] = total_ref[...] + branch


def feed_forward(layer, u, total, w, tables, steps):
    m = u.shape[0]
    wide = FF // steps
    block = pl.BlockSpec((m, wide), lambda g: (0, g))
    return pl.pallas_call(
        feed_forward_kernel,
        grid=(steps,),
        in_specs=[
            whole(m, D), whole(m, D), row_of(layer), row_of(layer),
            pl.BlockSpec((None, D, wide), lambda g: (layer, 0, g)),
            pl.BlockSpec((None, 1, wide), lambda g: (layer, 0, g)),
            pl.BlockSpec((None, wide, D), lambda g: (layer, g, 0)),
            row_of(layer), row_of(layer), whole(m, 1),
        ],
        out_specs=[whole(m, D), whole(m, D), whole(m, D), block, block, whole(m, D)],
        out_shape=[
            jax.ShapeDtypeStruct((m, D), BF16),
            jax.ShapeDtypeStruct((m, D), F32),
            jax.ShapeDtypeStruct((m, D), BF16),
            jax.ShapeDtypeStruct((m, FF), BF16),
            jax.ShapeDtypeStruct((m, FF), BF16),
            jax.ShapeDtypeStruct((m, D), BF16),
        ],
        scratch_shapes=[pltpu.VMEM((m, D), F32)],
        compiler_params=params(),
        cost_estimate=pl.CostEstimate(flops=8 * 10**9, bytes_accessed=20 * 10**6, transcendentals=10**6),
        name="feed_forward",
    )(
        u, total, w["forward_gain"], w["forward_shift"], w["hidden_weight"], w["hidden_bias"],
        w["return_weight"], w["return_bias"], w["forward_scale"], tables["live"],
    )


def feed_blocks(order_ref, bg_ref, scale_ref, live_ref, normed_ref, active_ref, slope_ref, wh_ref, wr_ref,
                dh_ref, dr_ref, hb_ref, ng_ref, out_ref, nt_ref, ot_ref):
    @pl.when(pl.program_id(0) == 0)
    def _():
        out = (bg_ref[...].astype(F32) * scale_ref[...] * live_ref[...]).astype(BF16)
        out_ref[...] = out
        ot_ref[...] = out.T
        nt_ref[...] = normed_ref[...].T

    dr_ref[...] = dot(ot_ref[...], active_ref[...]).astype(BF16)
    grad = dot(out_ref[...], wr_ref[...], NT) * slope_ref[...].astype(F32)
    grad = grad.astype(BF16)
    hb_ref[...] = column_sum(grad.astype(F32))
    dh_ref[...] = dot(nt_ref[...], grad).astype(BF16)
    ng_ref[...] += dot(grad, wh_ref[...], NT)


def feed_send_kernel(order_ref, bg_ref, scale_ref, live_ref, normed_ref, active_ref, slope_ref, wh_ref, wr_ref,
                     dh_ref, dr_ref, hb_ref, ng_ref, out_ref, nt_ref, ot_ref):
    @pl.when(pl.program_id(0) == 0)
    def _():
        ng_ref[...] = jnp.zeros_like(ng_ref)

    feed_blocks(order_ref, bg_ref, scale_ref, live_ref, normed_ref, active_ref, slope_ref, wh_ref, wr_ref,
                dh_ref, dr_ref, hb_ref, ng_ref, out_ref, nt_ref, ot_ref)


def feed_keep_kernel(order_ref, bg_ref, scale_ref, live_ref, normed_ref, active_ref, slope_ref, wh_ref, wr_ref,
                     part_ref, u_ref, gain_ref, branch_ref,
                     dh_ref, dr_ref, hb_ref, next_ref, small_ref, ng_ref, out_ref, nt_ref, ot_ref):
    @pl.when(pl.program_id(0) == 0)
    def _():
        ng_ref[...] = part_ref[...]

    feed_blocks(order_ref, bg_ref, scale_ref, live_ref, normed_ref, active_ref, slope_ref, wh_ref, wr_ref,
                dh_ref, dr_ref, hb_ref, ng_ref, out_ref, nt_ref, ot_ref)

    @pl.when(pl.program_id(0) == pl.num_programs(0) - 1)
    def _():
        whitened, inverse = norm_stats(u_ref[...].astype(F32))
        ng = ng_ref[...]
        bg = bg_ref[...].astype(F32)
        next_ref[...] = bg + norm_back(ng, whitened, inverse, gain_ref[...])
        small_ref[...] = jnp.zeros_like(small_ref)
        small_ref[0:1] = column_sum(ng * whitened)
        small_ref[1:2] = column_sum(ng)
        small_ref[2:3] = column_sum(out_ref[...].astype(F32))
        small_ref[3:4] = column_sum(bg * branch_ref[...].astype(F32) * live_ref[...])


def feed_backward(layer, order, sections, bg, saved, w, tables, keep=None):
    m = bg.shape[0]
    wide = FF // sections
    steps = sections // 2
    block = pl.BlockSpec((m, wide), lambda i, order: (0, order[i]))
    in_specs = [
        whole(m, D), row_of(layer), whole(m, 1), whole(m, D), block, block,
        pl.BlockSpec((None, D, wide), lambda i, order: (layer, 0, order[i])),
        pl.BlockSpec((None, wide, D), lambda i, order: (layer, order[i], 0)),
    ]
    operands = [bg, w["forward_scale"], tables["live"], saved["normed"], saved["active"], saved["slope"],
                w["hidden_weight"], w["return_weight"]]
    out_specs = [
        pl.BlockSpec((None, D, wide), lambda i, order: (i, 0, 0)),
        pl.BlockSpec((None, D, wide), lambda i, order: (i, 0, 0)),
        pl.BlockSpec((None, 1, wide), lambda i, order: (i, 0, 0)),
        whole(m, D),
    ]
    out_shape = [
        jax.ShapeDtypeStruct((steps, D, wide), BF16),
        jax.ShapeDtypeStruct((steps, D, wide), BF16),
        jax.ShapeDtypeStruct((steps, 1, wide), F32),
        jax.ShapeDtypeStruct((m, D), F32),
    ]
    scratch = [pltpu.VMEM((m, D), BF16), pltpu.VMEM((D, m), BF16), pltpu.VMEM((D, m), BF16)]
    kernel = feed_send_kernel
    if keep is not None:
        kernel = feed_keep_kernel
        in_specs += [whole(m, D), whole(m, D), row_of(layer), whole(m, D)]
        operands += [keep, saved["u"], w["forward_gain"], saved["branch"]]
        out_specs.append(whole(8, D))
        out_shape.append(jax.ShapeDtypeStruct((8, D), F32))
        scratch = [pltpu.VMEM((m, D), F32)] + scratch
    return pl.pallas_call(
        kernel,
        grid_spec=pltpu.PrefetchScalarGridSpec(
            num_scalar_prefetch=1, grid=(steps,), in_specs=in_specs, out_specs=out_specs, scratch_shapes=scratch
        ),
        out_shape=out_shape,
        compiler_params=params(),
        cost_estimate=pl.CostEstimate(flops=8 * 10**9, bytes_accessed=15 * 10**6, transcendentals=0),
        name="feed_send" if keep is None else "feed_keep",
    )(order, *operands)


def attention_backward_kernel(
    images, u_ref, bg_ref, gain_ref, scale_ref, live_ref, q_ref, k_ref, v_ref, w_ref, branch_ref,
    wq_ref, wk_ref, wv_ref, wo_ref, p_ref, st_ref,
    next_ref, out_ref, gq_ref, gk_ref, gv_ref, table_ref, bias_ref, small_ref,
    ng_ref, even_ref, odd_ref,
):
    step = pl.program_id(0)

    @pl.when(step == 0)
    def _():
        out_ref[...] = (bg_ref[...] * scale_ref[...] * live_ref[...]).astype(BF16)
        ng_ref[...] = jnp.zeros_like(ng_ref)

    att_grad = dot(out_ref[...], wo_ref[...], NT).astype(BF16)
    masks = head_masks()
    for pair in range(QUAD // 2):
        lanes = slice(128 * pair, 128 * pair + 128)
        even_ref[...] = jnp.zeros_like(even_ref)
        odd_ref[...] = jnp.zeros_like(odd_ref)
        for n in range(images):
            rows = slice(RP * n, RP * n + RP)
            qn, kn, vn = q_ref[rows, lanes], k_ref[rows, lanes], v_ref[rows, lanes]
            an = att_grad[rows, lanes]
            dq = dk = dv = None
            for e in range(2):
                weights = w_ref[n, 2 * pair + e]
                chosen = an * masks[e]
                weights_grad = dot(chosen, vn, NT)
                probs = weights.astype(F32)
                product = weights_grad * probs
                score_grad = (product - probs * jnp.sum(product, axis=1, keepdims=True)).astype(BF16)
                parts = (
                    dot(score_grad, kn * masks[e]),
                    dot(score_grad, qn * masks[e], TN),
                    dot(weights, chosen, TN),
                )
                dq, dk, dv = parts if dq is None else (dq + parts[0], dk + parts[1], dv + parts[2])
                moved = dot(p_ref[n], score_grad).astype(BF16)
                spread = dot(moved, st_ref[n])
                for a in range(0, HMAX, 2):
                    at = slice(PITCH * a, PITCH * a + COLK)
                    even_ref[e, :, at] += spread[WMAX * a : WMAX * a + WMAX]
                    odd_ref[e, :, at] += spread[WMAX * a + WMAX : WMAX * a + 2 * WMAX]
            gq_ref[rows, lanes] = (dq.astype(BF16).astype(F32) * 0.125).astype(BF16)
            gk_ref[rows, lanes] = dk.astype(BF16)
            gv_ref[rows, lanes] = dv.astype(BF16)
        for e in range(2):
            both = even_ref[e] + pltpu.roll(odd_ref[e], PITCH, 1)
            table_ref[2 * pair + e] = column_sum(pltpu.roll(both, 0, 1, stride=1, stride_axis=0))
    gq, gk, gv = gq_ref[...], gk_ref[...], gv_ref[...]
    bias_ref[0] = column_sum(gq.astype(F32))
    bias_ref[1] = column_sum(gv.astype(F32))
    ng_ref[...] += dot(gq, wq_ref[...], NT) + dot(gk, wk_ref[...], NT) + dot(gv, wv_ref[...], NT)

    @pl.when(step == pl.num_programs(0) - 1)
    def _():
        whitened, inverse = norm_stats(u_ref[...].astype(F32))
        ng = ng_ref[...]
        bg = bg_ref[...]
        next_ref[...] = bg + norm_back(ng, whitened, inverse, gain_ref[...])
        small_ref[...] = jnp.zeros_like(small_ref)
        small_ref[0:1] = column_sum(ng * whitened)
        small_ref[1:2] = column_sum(ng)
        small_ref[2:3] = column_sum(out_ref[...].astype(F32))
        small_ref[3:4] = column_sum(bg * branch_ref[...].astype(F32) * live_ref[...])


def attention_backward(layer, images, bg, saved, w, tables):
    m = bg.shape[0]
    wide = QUAD * HEAD
    steps = HEADS // QUAD
    block = pl.BlockSpec((m, wide), lambda g: (0, g))
    third = lambda which: pl.BlockSpec((None, D, wide), lambda g: (layer, 0, which * steps + g))
    return pl.pallas_call(
        functools.partial(attention_backward_kernel, images),
        grid=(steps,),
        in_specs=[
            whole(m, D), whole(m, D), row_of(layer), row_of(layer), whole(m, 1), block, block, block,
            pl.BlockSpec((images, QUAD, RP, RP), lambda g: (0, g, 0, 0)),
            whole(m, D), third(0), third(1), third(2),
            pl.BlockSpec((None, wide, D), lambda g: (layer, g, 0)),
            whole(images, ROWK, RP), whole(images, RP, COLK),
        ],
        out_specs=[
            whole(m, D), whole(m, D), block, block, block,
            pl.BlockSpec((QUAD, 1, TABW), lambda g: (g, 0, 0)),
            pl.BlockSpec((2, 1, wide), lambda g: (0, 0, g)),
            whole(8, D),
        ],
        out_shape=[
            jax.ShapeDtypeStruct((m, D), F32),
            jax.ShapeDtypeStruct((m, D), BF16),
            jax.ShapeDtypeStruct((m, D), BF16),
            jax.ShapeDtypeStruct((m, D), BF16),
            jax.ShapeDtypeStruct((m, D), BF16),
            jax.ShapeDtypeStruct((HEADS, 1, TABW), F32),
            jax.ShapeDtypeStruct((2, 1, D), F32),
            jax.ShapeDtypeStruct((8, D), F32),
        ],
        scratch_shapes=[
            pltpu.VMEM((m, D), F32), pltpu.VMEM((2, WMAX, TABW), F32), pltpu.VMEM((2, WMAX, TABW), F32),
        ],
        compiler_params=params(),
        cost_estimate=pl.CostEstimate(flops=16 * 10**9, bytes_accessed=15 * 10**6, transcendentals=0),
        name="attention_backward",
    )(
        saved["u"], bg, w["attention_gain"], w["attention_scale"], tables["live"], saved["q"], saved["k"], saved["v"],
        saved["w"], saved["branch"], w["input_projection"], w["input_projection"], w["input_projection"],
        w["output_projection"], tables["p"], tables["st"],
    )


def attention_weights_kernel(order_ref, normed_ref, att_ref, grads_ref, out_ref, nt_ref, at_ref):
    @pl.when(pl.program_id(0) == 0)
    def _():
        nt_ref[...] = normed_ref[...].T
        at_ref[...] = att_ref[...].T

    first = 3 * D // (4 * 128) * 128
    low = lax.broadcasted_iota(jnp.int32, (1, 128), 1) < HEAD
    left = dot(nt_ref[...], grads_ref[:, : first + 128])
    right = dot(at_ref[...], grads_ref[:, first:])
    out_ref[:, :first] = left[:, :first].astype(BF16)
    out_ref[:, first : first + 128] = jnp.where(low, left[:, first:], right[:, :128]).astype(BF16)
    out_ref[:, first + 128 :] = right[:, 128:].astype(BF16)


def attention_weights(order, sections, saved, grads):
    m = grads.shape[1]
    steps = sections // 2
    return pl.pallas_call(
        attention_weights_kernel,
        grid_spec=pltpu.PrefetchScalarGridSpec(
            num_scalar_prefetch=1,
            grid=(steps,),
            in_specs=[
                whole(m, D), whole(m, D), pl.BlockSpec((None, m, D), lambda i, order: (order[i], 0, 0)),
            ],
            out_specs=pl.BlockSpec((None, D, D), lambda i, order: (i, 0, 0)),
            scratch_shapes=[pltpu.VMEM((D, m), BF16), pltpu.VMEM((D, m), BF16)],
        ),
        out_shape=jax.ShapeDtypeStruct((steps, D, D), BF16),
        compiler_params=params(),
        cost_estimate=pl.CostEstimate(flops=2 * 10**9, bytes_accessed=5 * 10**6, transcendentals=0),
        name="attention_weights",
    )(order, saved["normed"], saved["attended"], grads)


def flip(value, axis, bit):
    count = lax.axis_size(axis)
    return lax.ppermute(value, axis, [(i, i ^ bit) for i in range(count)])


def bits_of(axis):
    return [1 << i for i in range(lax.axis_size(axis).bit_length() - 1)]


def own_bit(axis, bit):
    return (lax.axis_index(axis) // bit) % 2


def sum_up(terms):
    total = terms[0].astype(F32)
    for term in terms[1:]:
        total = total + term.astype(F32)
    return total


def halvings(keep, received, order):
    section_bits = [("section", bit) for bit in reversed(bits_of("section")[1:])]
    wide_bits = [("wide", bit) for bit in reversed(bits_of("wide"))]
    names = section_bits + wide_bits
    shape = (2,) * len(names) + (D // lax.axis_size("wide"),) + keep.shape[2:]
    terms = [keep.reshape(shape), received.reshape(shape)]
    for name in order:
        at = names.index(name)
        names = names[:at] + names[at + 1 :]
        mine = own_bit(*name)
        take = lambda term, which: lax.dynamic_index_in_dim(term, which, at, keepdims=False)
        going = sum_up([take(term, 1 - mine) for term in terms]).astype(BF16)
        terms = [take(term, mine) for term in terms] + [flip(going, *name)]
    return sum_up(terms)


def orders():
    section_bits = [("section", bit) for bit in bits_of("section")[1:]]
    wide_bits = [("wide", bit) for bit in bits_of("wide")]
    return section_bits + wide_bits, wide_bits[:1] + section_bits + wide_bits[1:]


def small_total(parts):
    value = parts
    for bit in reversed(bits_of("section")):
        value = value.reshape((2, -1) + value.shape[1:])
        mine = own_bit("section", bit)
        other = flip(lax.dynamic_index_in_dim(value, 1 - mine, 0, keepdims=False), "section", bit)
        value = lax.dynamic_index_in_dim(value, mine, 0, keepdims=False) + other
    for bit in bits_of("wide"):
        value = value + flip(value, "wide", bit)
    return value[0]


def redistribute(rows, sections):
    me = lax.axis_index("section")
    images = rows.shape[0]
    width = D // sections
    cut = lambda s: lax.dynamic_slice_in_dim(rows, s * width, width, 2)
    result = jnp.zeros((sections * images, ROWS, width), rows.dtype)
    for distance in range(sections):
        piece = cut(me ^ distance)
        if distance:
            piece = flip(piece, "section", distance)
        result = lax.dynamic_update_slice_in_dim(result, piece, (me ^ distance) * images, 0)
    return result


def on_device(
    tokens, cotangent, patch_grids, attention_gain, attention_shift, input_projection, query_bias, value_bias,
    relative_table, output_projection, output_bias, attention_scale, forward_gain, forward_shift, hidden_weight,
    hidden_bias, return_weight, return_bias, forward_scale,
):
    sections = lax.axis_size("section")
    me = lax.axis_index("section")
    images = tokens.shape[0] // sections
    m = images * RP
    row = lambda v: v.reshape(LAYERS, 1, -1)
    w = {
        "attention_gain": row(attention_gain), "attention_shift": row(attention_shift),
        "input_projection": input_projection, "query_bias": row(query_bias), "value_bias": row(value_bias),
        "output_projection": output_projection, "output_bias": row(output_bias),
        "attention_scale": row(attention_scale), "forward_gain": row(forward_gain),
        "forward_shift": row(forward_shift), "hidden_weight": hidden_weight, "hidden_bias": row(hidden_bias),
        "return_weight": return_weight, "return_bias": row(return_bias), "forward_scale": row(forward_scale),
    }

    def mine(v):
        part = lax.dynamic_slice_in_dim(v, me * images, images, 0)
        return jnp.pad(part, ((0, 0), (0, RP - ROWS), (0, 0))).reshape(m, D)

    u = mine(tokens)
    cot = mine(cotangent)
    grids = lax.dynamic_slice_in_dim(patch_grids, me * images, images, 0)

    place = lax.broadcasted_iota(jnp.int32, (images, RP), 1)
    height, width = grids[:, 0:1], grids[:, 1:2]
    a, b = place // width, place % width
    live = place < height * width
    row_forward = jnp.where(live, a * WMAX + (WMAX - 1) - b, -1)
    row_backward = jnp.where(live, a * WMAX + b, -1)
    column = jnp.where(live, (HMAX - 1 - a) * PITCH + (WMAX - 1) - b, -1)
    pick = lambda index, count: (index[:, :, None] == lax.broadcasted_iota(jnp.int32, (1, 1, count), 2)).astype(BF16)
    pick_t = lambda index, count: (index[:, None, :] == lax.broadcasted_iota(jnp.int32, (1, count, 1), 1)).astype(BF16)
    table = jnp.transpose(relative_table.reshape(LAYERS, 2 * HMAX - 1, QW, HEADS), (0, 3, 1, 2))
    table = jnp.pad(table, ((0, 0), (0, 0), (0, 1), (0, PITCH - QW))).reshape(LAYERS, HEADS, 1, TABW)
    table = jnp.roll(table, -(WMAX - 1), axis=3)
    tables = {
        "live": live.reshape(m, 1).astype(F32),
        "mask": jnp.where(live, 0.0, -1e9).astype(F32).reshape(images, 1, RP),
        "s": pick_t(column, COLK),
        "st": pick(column, COLK),
        "pt": pick(row_forward, ROWK),
        "p": pick_t(row_backward, ROWK),
        "table": table,
    }

    total = u.astype(F32)
    kept_attention, kept_feed = [], []
    for layer in range(LAYERS):
        later, total, normed, q, k, v, attended, weights, branch = attention_forward(layer, images, u, total, w, tables)
        kept_attention.append(dict(u=u, normed=normed, q=q, k=k, v=v, attended=attended, w=weights, branch=branch))
        u = later
        later, total, normed, active, slope, branch = feed_forward(layer, u, total, w, tables, sections)
        kept_feed.append(dict(u=u, normed=normed, active=active, slope=slope, branch=branch))
        u = later
    layer_output = redistribute(total.reshape(images, RP, D)[:, :ROWS].astype(BF16), sections)

    core = me % 2
    sent = jnp.arange(sections // 2, dtype=jnp.int32) * 2 + (1 - core)
    kept = jnp.arange(sections // 2, dtype=jnp.int32) * 2 + core
    first, second = orders()
    bg = cot.astype(F32)
    hidden_grads, return_grads, projection_grads, out_grads, smalls = ([None] * LAYERS for _ in range(5))
    for layer in reversed(range(LAYERS)):
        saved = kept_feed[layer]
        dh_send, dr_send, hb_send, part = feed_backward(layer, sent, sections, bg, saved, w, tables)
        dh_got, dr_got = flip(dh_send, "section", 1), flip(dr_send, "section", 1)
        dh_keep, dr_keep, hb_keep, bg, feed_small = feed_backward(
            layer, kept, sections, bg, saved, w, tables, keep=part
        )
        hidden_grads[layer] = halvings(dh_keep, dh_got, first)
        return_grads[layer] = halvings(dr_keep, dr_got, second)
        hidden_shift = jnp.zeros((sections // 2, 2, FF // sections), F32)
        hidden_shift = lax.dynamic_update_slice_in_dim(hidden_shift, hb_send, 1 - core, 1)
        hidden_shift = lax.dynamic_update_slice_in_dim(hidden_shift, hb_keep, core, 1)

        saved = kept_attention[layer]
        bg, out_rows, gq, gk, gv, table_grad, biases, attention_small = attention_backward(
            layer, images, bg, saved, w, tables
        )
        projected = jnp.concatenate([gq, gk, gv], axis=1)
        part = 3 * D // sections
        grads = jnp.stack([
            jnp.concatenate(
                [projected[:, part * s : part * s + part], out_rows[:, D // sections * s : D // sections * (s + 1)]],
                axis=1,
            )
            for s in range(sections)
        ])
        da_send = attention_weights(sent, sections, saved, grads)
        da_got = flip(da_send, "section", 1)
        da_keep = attention_weights(kept, sections, saved, grads)
        half = D // 2
        da = jnp.concatenate([
            halvings(da_keep[:, :, :half], da_got[:, :, :half], first),
            halvings(da_keep[:, :, half:], da_got[:, :, half:], second),
        ], axis=1)
        projection_grads[layer], out_grads[layer] = da[:, :part], da[:, part:]
        vectors = jnp.concatenate([attention_small[:4], feed_small[:4], biases[:, 0]], axis=0)
        vectors = jnp.transpose(vectors.reshape(10, sections, D // sections), (1, 0, 2)).reshape(sections, -1)
        packed = jnp.concatenate(
            [vectors, hidden_shift.reshape(sections, -1), table_grad.reshape(sections, -1)], axis=1
        )
        smalls[layer] = small_total(packed)
    input_grad = redistribute(bg.reshape(images, RP, D)[:, :ROWS].astype(BF16), sections)

    small = jnp.stack(smalls)
    each = D // sections
    vector = lambda i: small[:, i * each : (i + 1) * each]
    hidden_shift = small[:, 10 * each : 10 * each + FF // sections]
    table_grad = small[:, 10 * each + FF // sections :].reshape(LAYERS, HEADS // sections, 2 * HMAX, PITCH)
    table_grad = table_grad[:, :, : 2 * HMAX - 1, :QW].reshape(LAYERS, HEADS // sections, REL)
    return (
        layer_output, input_grad,
        vector(0), vector(1), jnp.stack(projection_grads), vector(8), vector(9),
        jnp.transpose(table_grad, (0, 2, 1)), jnp.stack(out_grads), vector(2), vector(3),
        vector(4), vector(5), jnp.stack(hidden_grads), hidden_shift,
        jnp.transpose(jnp.stack(return_grads), (0, 2, 1)), vector(6), vector(7),
    )


def solution(mesh):
    three, two = P("wide", None, "section"), P(None, "section")
    weight = P(None, "wide", "section")
    return jax.shard_map(
        on_device,
        mesh=mesh,
        in_specs=(P("wide", None, None), P("wide", None, None), P("wide", None)) + (P(),) * 16,
        out_specs=(
            three, three, two, two, weight, two, two, P(None, None, "section"), weight, two, two, two, two,
            weight, two, P(None, "section", "wide"), two, two,
        ),
        check_vma=False,
    )
```

time: 6030 us -> 499 us (0.08)
  other arithmetic: 2130 us -> 52.9 us
  local copies, waits for them, and re-layouts: 2030 us -> 51.3 us
  waiting for transfers between devices: 1250 us -> 125 us
  matrix products: 311 us -> 0 us
  Pallas kernels: 0 us -> 185 us
  starting transfers between devices: 176 us -> 73.4 us
    scatter-add x8 -> x0, other arithmetic: 1730 us -> none  [attention_backward(): jax.ops.segment_sum(flat_scores, rel_index.reshape(-1), num_segments=REL)]
    gather x32 -> x0, local copies, waits for them, and re-layouts: 1410 us -> none  [masked_scores(): jnp.take(bias_table, rel_index, axis=0)]
    reduce_scatter x8 -> x0, waiting for transfers between devices: 590 us -> none  [the longest x1 164 us: on_device(): lax.psum_scatter(return_sum, 'wide', scatter_dimension=1, tiled=True)]
    dot_general x128 -> x0, matrix products: 311 us -> none  [the longest x16 90.4 us: outer_sum(): jnp.einsum('nrd,nre->de', left, right, preferred_element_type=jnp.float32)]
    ppermute x22 -> x54, waiting for transfers between devices: 391 us -> 125 us  [flip(): return lax.ppermute(value, axis, [(i, i ^ bit) for i in range(count)])]
    unnamed x34 -> x0, waiting for transfers between devices: 265 us -> none
    pallas_call x0 -> x14, Pallas kernels: none -> 185 us  [the longest x2 48.3 us: attention_backward(): pl.pallas_call(functools.partial(attention_backward_kernel, images), grid...]
    add x200 -> x16, other arithmetic: 183 us -> 4.53 us  [the longest x4 2.47 us: small_total(): value = lax.dynamic_index_in_dim(value, mine, 0, keepdims=False) + other]
  transfers between devices with their start and end apart: 43 -> 54, of which waited for: 30 -> 29; matrix products, arithmetic and copies ran while one was open for 3% -> 17% of each run, Pallas kernels for 0% -> 4%
where the time goes in v1:
time: 499 us; the launch traced here: 490 us
  Pallas kernels  185 us (37%)
  waiting for transfers between devices  125 us (25%)
  starting transfers between devices  73.4 us (15%)
  other arithmetic  52.9 us (11%)
  local copies, waits for them, and re-layouts  51.3 us (10%)
    ppermute x54, waiting for transfers between devices, flip(): return lax.ppermute(value, axis, [(i, i ^ bit) for i in range(count)])  125 us
    ppermute x54, starting transfers between devices, flip(): return lax.ppermute(value, axis, [(i, i ^ bit) for i in range(count)])  73.4 us
    pallas_call x2, Pallas kernels, attention_backward(): pl.pallas_call(functools.partial(attention_backward_kernel, images), grid...  48.3 us
    pallas_call x2, Pallas kernels, attention_forward(): pl.pallas_call(functools.partial(attention_forward_kernel, images), grid=...  47.3 us
    pallas_call x4, Pallas kernels, feed_backward(): pl.pallas_call(kernel, grid_spec=pltpu.PrefetchScalarGridSpec(num_scalar_...  44.1 us
    pallas_call x2, Pallas kernels, feed_forward(): pl.pallas_call(feed_forward_kernel, grid=(steps,), in_specs=[whole(m, D),...  24.1 us
    convert_element_type x32, other arithmetic, halvings(): going = sum_up([take(term, 1 - mine) for term in terms]).astype(BF16)  22.1 us
    unnamed x96, local copies, waits for them, and re-layouts  21.2 us
  transfers between devices with their start and end apart: 54, of which 29 were waited for; matrix products, arithmetic and copies ran while one was open for 17% of the time, Pallas kernels for 4%

profile of v1, /device:TPU:0, one launch (start us, length us, event | category | flops | bytes accessed | tf_op | source)
XLA Modules:
  0.0 490.0 jit_solution(4223719179319818660)
XLA Ops:
  11.1 23.4 %attention_forward.2 = (bf16[416,768]{1,0:T(8,128)(2,1)S(1)}, f32[416,768]{1,0:T(8,128)}, bf16[416,768]{1,0:T(8,128)(2,1)}, bf16[416,768]{1,0:T(8,128)(2,1)}, bf...) custom-call(bf16[416,768]{1,0:T(8,128)(2,1)} %bitcast.504, ...), custom_call_target="tpu_custom_call" | custom-call | flops 12000000000 | bytes 15000000 | tf_op jit(solution)/shard_map/attention_forward/pallas_call | solution.py:152
  35.4 11.9 %feed_forward.2 = (bf16[416,768]{1,0:T(8,128)(2,1)S(1)}, f32[416,768]{1,0:T(8,128)}, bf16[416,768]{1,0:T(8,128)(2,1)S(1)}, bf16[416,3072]{1,0:T(8,128)(2,1)}, bf...) custom-call(bf16[416,768]{1,0:T(8,128)(2,1)} %copy-done.2, f32[416,768]{1,0:T(8,128)} %get-tuple-element.82.total_ref, ...), custom_call_target="tpu_custom_call" | custom-call | flops 8000000000 | bytes 20000000 | tf_op jit(solution)/shard_map/feed_forward/pallas_call | solution.py:212
  48.2 23.8 %attention_forward.3 = (bf16[416,768]{1,0:T(8,128)(2,1)S(1)}, f32[416,768]{1,0:T(8,128)}, bf16[416,768]{1,0:T(8,128)(2,1)}, bf16[416,768]{1,0:T(8,128)(2,1)}, bf...) custom-call(bf16[416,768]{1,0:T(8,128)(2,1)} %copy-done.10, ...), custom_call_target="tpu_custom_call" | custom-call | flops 12000000000 | bytes 15000000 | tf_op jit(solution)/shard_map/attention_forward/pallas_call | solution.py:152
  72.9 12.2 %feed_forward.3 = (bf16[416,768]{1,0:T(8,128)(2,1)}, f32[416,768]{1,0:T(8,128)}, bf16[416,768]{1,0:T(8,128)(2,1)S(1)}, bf16[416,3072]{1,0:T(8,128)(2,1)}, bf16[4...) custom-call(bf16[416,768]{1,0:T(8,128)(2,1)} %copy-done.4, f32[416,768]{1,0:T(8,128)} %get-tuple-element.86.total_ref, ...), custom_call_target="tpu_custom_call" | custom-call | flops 8000000000 | bytes 20000000 | tf_op jit(solution)/shard_map/feed_forward/pallas_call | solution.py:212
  85.0 9.8 %feed_send.2 = (bf16[2,768,768]{2,1,0:T(8,128)(2,1)}, bf16[2,768,768]{2,1,0:T(8,128)(2,1)}, f32[2,1,768]{2,1,0:T(1,128)S(1)}, f32[416,768]{1,0:T(8,128)}) custom-call(s32[2]{0:T(128)S(1)} %fusion.76.order_ref, f32[416,768]{1,0:T(8,128)} %bitcast_convert_fusion.bg_ref, f32[2,1,768]{2,1,0:T(1,128)S(1)} %reshape.1366.scale_ref, ...), custom_call_target="tpu_custom_call" | custom-call | flops 8000000000 | bytes 15000000 | tf_op jit(solution)/shard_map/feed_send/pallas_call | solution.py:324
  94.8 12.3 %feed_keep.2 = (bf16[2,768,768]{2,1,0:T(8,128)(2,1)}, bf16[2,768,768]{2,1,0:T(8,128)(2,1)}, f32[2,1,768]{2,1,0:T(1,128)S(1)}, f32[416,768]{1,0:T(8,128)}, f32[8,768]{1,0:T(8,128)S(1)}) custom-call(s32[2]{0:T(128)S(1)} %fusion.77.order_ref, f32[416,768]{1,0:T(8,128)} %bitcast_convert_fusion.bg_ref, f32[2,1,768]{2,1,0:T(1,128)S(1)} %reshape.1366.scale_ref, ...), custom_call_target="tpu_custom_call" | custom-call | flops 8000000000 | bytes 15000000 | tf_op jit(solution)/shard_map/feed_keep/pallas_call | solution.py:324
  107.1 24.1 %attention_backward.2 = (f32[416,768]{1,0:T(8,128)}, bf16[416,768]{1,0:T(8,128)(2,1)S(1)}, bf16[416,768]{1,0:T(8,128)(2,1)S(1)}, bf16[416,768]{1,0:T(8,128)(2,1)...) custom-call(bf16[416,768]{1,0:T(8,128)(2,1)} %copy-done.10, ...), custom_call_target="tpu_custom_call" | custom-call | flops 16000000000 | bytes 15000000 | tf_op jit(solution)/shard_map/attention_backward/pallas_call | solution.py:409
  131.2 10.0 %feed_send.3 = (bf16[2,768,768]{2,1,0:T(8,128)(2,1)}, bf16[2,768,768]{2,1,0:T(8,128)(2,1)}, f32[2,1,768]{2,1,0:T(1,128)S(1)}, f32[416,768]{1,0:T(8,128)}) custom-call(s32[2]{0:T(128)S(1)} %fusion.76.order_ref, f32[416,768]{1,0:T(8,128)} %get-tuple-element.99.bg_ref, f32[2,1,768]{2,1,0:T(1,128)S(1)} %reshape.1366.scale_ref, f32[416,1]{1,0:T(8,128)S(1)} %reshape.1461.live_ref, ...), custom_call_target="tpu_custom_call" | custom-call | flops 8000000000 | bytes 15000000 | tf_op jit(solution)/shard_map/feed_send/pallas_call | solution.py:324
  141.2 12.1 %feed_keep.3 = (bf16[2,768,768]{2,1,0:T(8,128)(2,1)}, bf16[2,768,768]{2,1,0:T(8,128)(2,1)}, f32[2,1,768]{2,1,0:T(1,128)S(1)}, f32[416,768]{1,0:T(8,128)}, f32[8,768]{1,0:T(8,128)S(1)}) custom-call(s32[2]{0:T(128)S(1)} %fusion.77.order_ref, f32[416,768]{1,0:T(8,128)} %get-tuple-element.99.bg_ref, f32[2,1,768]{2,1,0:T(1,128)S(1)} %reshape.1366.scale_ref, ...), custom_call_target="tpu_custom_call" | custom-call | flops 8000000000 | bytes 15000000 | tf_op jit(solution)/shard_map/feed_keep/pallas_call | solution.py:324
  153.3 24.2 %attention_backward.3 = (f32[416,768]{1,0:T(8,128)}, bf16[416,768]{1,0:T(8,128)(2,1)S(1)}, bf16[416,768]{1,0:T(8,128)(2,1)S(1)}, bf16[416,768]{1,0:T(8,128)(2,1)...) custom-call(bf16[416,768]{1,0:T(8,128)(2,1)} %bitcast.505, ...), custom_call_target="tpu_custom_call" | custom-call | flops 16000000000 | bytes 15000000 | tf_op jit(solution)/shard_map/attention_backward/pallas_call | solution.py:409
  188.4 5.6 %attention_weights.5 = bf16[2,768,768]{2,1,0:T(8,128)(2,1)} custom-call(s32[2]{0:T(128)S(1)} %fusion.76.order_ref, bf16[416,768]{1,0:T(8,128)(2,1)S(1)} %copy-done.6, bf16[416,768]{1,0:T(8,128)(2,1)S(1)} %copy-done.7, bf16[4,416,768]{2,1,0:T(8,128)(2,1)} %pad_maximum_fusion.grads_ref), custom_call_target="tpu_custom_call" | custom-call | flops 2000000000 | bytes 5000000 | tf_op jit(solution)/shard_map/attention_weights/pallas_call | solution.py:466
  198.7 5.1 %attention_weights.7 = bf16[2,768,768]{2,1,0:T(8,128)(2,1)} custom-call(s32[2]{0:T(128)S(1)} %fusion.76.order_ref, bf16[416,768]{1,0:T(8,128)(2,1)S(1)} %copy-done.8, bf16[416,768]{1,0:T(8,128)(2,1)S(1)} %copy-done.9, bf16[4,416,768]{2,1,0:T(8,128)(2,1)} %pad_maximum_fusion.1.grads_ref), custom_call_target="tpu_custom_call" | custom-call | flops 2000000000 | bytes 5000000 | tf_op jit(solution)/shard_map/attention_weights/pallas_call | solution.py:466
  207.8 5.1 %attention_weights.4 = bf16[2,768,768]{2,1,0:T(8,128)(2,1)} custom-call(s32[2]{0:T(128)S(1)} %fusion.77.order_ref, bf16[416,768]{1,0:T(8,128)(2,1)S(1)} %copy-done.6, bf16[416,768]{1,0:T(8,128)(2,1)S(1)} %copy-done.7, bf16[4,416,768]{2,1,0:T(8,128)(2,1)} %pad_maximum_fusion.grads_ref), custom_call_target="tpu_custom_call" | custom-call | flops 2000000000 | bytes 5000000 | tf_op jit(solution)/shard_map/attention_weights/pallas_call | solution.py:466
  212.9 5.4 %attention_weights.6 = bf16[2,768,768]{2,1,0:T(8,128)(2,1)} custom-call(s32[2]{0:T(128)S(1)} %fusion.77.order_ref, bf16[416,768]{1,0:T(8,128)(2,1)S(1)} %copy-done.8, bf16[416,768]{1,0:T(8,128)(2,1)S(1)} %copy-done.9, bf16[4,416,768]{2,1,0:T(8,128)(2,1)} %pad_maximum_fusion.1.grads_ref), custom_call_target="tpu_custom_call" | custom-call | flops 2000000000 | bytes 5000000 | tf_op jit(solution)/shard_map/attention_weights/pallas_call | solution.py:466
  312.8 11.5 %collective-permute-done.30 = bf16[2,2,2,96,384]{4,3,2,1,0:T(8,128)(2,1)S(1)} collective-permute-done((bf16[2,2,2,96,384]{4,3,2,1,0:T(8,128)(2,1)S(1)}, bf16[2,2,2,96,384]{4,3,2,1,0:T(8,128)(2,1)S(1)}, u32[]{:S(2)}, u32[]{:S(2)}) %collective-permute-start.30) | collective-permute-done | bytes 589856 | tf_op jit(solution)/shard_map/ppermute | solution.py:486
  332.1 5.2 %collective-permute-done.22 = bf16[2,2,96,384]{3,2,1,0:T(8,128)(2,1)S(1)} collective-permute-done((bf16[2,2,96,384]{3,2,1,0:T(8,128)(2,1)S(1)}, bf16[2,2,96,384]{3,2,1,0:T(8,128)(2,1)S(1)}, u32[]{:S(2)}, u32[]{:S(2)}) %collective-permute-start.22) | collective-permute-done | bytes 294944 | tf_op jit(solution)/shard_map/ppermute | solution.py:486
  338.3 4.5 collective-permute-done.31
  344.7 36.5 %collective-permute-done.18 = bf16[2,2,96,384]{3,2,1,0:T(8,128)(2,1)S(1)} collective-permute-done((bf16[2,2,96,384]{3,2,1,0:T(8,128)(2,1)S(1)}, bf16[2,2,96,384]{3,2,1,0:T(8,128)(2,1)S(1)}, u32[]{:S(2)}, u32[]{:S(2)}) %collective-permute-start.18) | collective-permute-done | bytes 294944 | tf_op jit(solution)/shard_map/ppermute | solution.py:486
  389.4 4.5 collective-permute-done.32
  427.3 4.5 collective-permute-start.36
  443.3 5.1 %collective-permute-done.51 = bf16[2,2,96,768]{3,2,1,0:T(8,128)(2,1)S(1)} collective-permute-done((bf16[2,2,96,768]{3,2,1,0:T(8,128)(2,1)S(1)}, bf16[2,2,96,768]{3,2,1,0:T(8,128)(2,1)S(1)}, u32[]{:S(2)}, u32[]{:S(2)}) %collective-permute-start.51) | collective-permute-done | bytes 589856 | tf_op jit(solution)/shard_map/ppermute | solution.py:486
  459.5 4.8 collective-permute-done.52
  467.2 5.4 %collective-permute-done.37 = bf16[2,96,768]{2,1,0:T(8,128)(2,1)S(1)} collective-permute-done((bf16[2,96,768]{2,1,0:T(8,128)(2,1)S(1)}, bf16[2,96,768]{2,1,0:T(8,128)(2,1)S(1)}, u32[]{:S(2)}, u32[]{:S(2)}) %collective-permute-start.37) | collective-permute-done | bytes 294944 | tf_op jit(solution)/shard_map/ppermute | solution.py:486
  479.9 6.2 %collective-permute-done.38 = bf16[96,768]{1,0:T(8,128)(2,1)S(1)} collective-permute-done((bf16[96,768]{1,0:T(8,128)(2,1)S(1)}, bf16[96,768]{1,0:T(8,128)(2,1)S(1)}, u32[]{:S(2)}, u32[]{:S(2)}) %collective-permute-start.38) | collective-permute-done | bytes 147488 | tf_op jit(solution)/shard_map/ppermute | solution.py:486
  (368 shorter events, 214.7 us)
Async XLA Ops:
  179.1 52.1 %collective-permute-start.6 = (f32[2,8064]{1,0:T(2,128)}, f32[2,8064]{1,0:T(2,128)}, u32[]{:S(2)}, u32[]{:S(2)}) collective-permute-start(f32[2,8064]{1,0:T(2,128)} %dynamic-slice_bitcast_fusion.1), channel_id=1, source_target_pairs={{0,2},{1,3},{2,0},{3,1},{4,6},{5,7},{6,4},{7,5},{8,10},{9,11},{10,... | collective-permute-start | bytes 193544 | tf_op jit(solution)/shard_map/ppermute | solution.py:486
  183.6 49.0 %collective-permute-start.11 = (f32[2,8064]{1,0:T(2,128)}, f32[2,8064]{1,0:T(2,128)}, u32[]{:S(2)}, u32[]{:S(2)}) collective-permute-start(f32[2,8064]{1,0:T(2,128)} %dynamic-slice_bitcast_fusion), channel_id=1, source_target_pairs={{0,2},{1,3},{2,0},{3,1},{4,6},{5,7},{6,4},{7,5},{8,10},{9,11},{10,... | collective-permute-start | bytes 193544 | tf_op jit(solution)/shard_map/ppermute | solution.py:486
  193.9 89.4 %collective-permute-start.16 = (bf16[2,768,768]{2,1,0:T(8,128)(2,1)}, bf16[2,768,768]{2,1,0:T(8,128)(2,1)}, u32[]{:S(2)}, u32[]{:S(2)}) collective-permute-start(bf16[2,768,768]{2,1,0:T(8,128)(2,1)} %attention_weights.5), channel_id=1, source_target_pairs={{0,1},{1,0},{2,3},{3,2},{4,5},{5,4},{6,7},{7,6},{8,9},{9,8},{10,11... | collective-permute-start | bytes 7077896 | tf_op jit(solution)/shard_map/ppermute | solution.py:486
  203.8 91.6 %collective-permute-start.25 = (bf16[2,768,768]{2,1,0:T(8,128)(2,1)}, bf16[2,768,768]{2,1,0:T(8,128)(2,1)}, u32[]{:S(2)}, u32[]{:S(2)}) collective-permute-start(bf16[2,768,768]{2,1,0:T(8,128)(2,1)} %attention_weights.7), channel_id=1, source_target_pairs={{0,1},{1,0},{2,3},{3,2},{4,5},{5,4},{6,7},{7,6},{8,9},{9,8},{10,11... | collective-permute-start | bytes 7077896 | tf_op jit(solution)/shard_map/ppermute | solution.py:486
  207.8 45.7 %collective-permute-start.3 = (bf16[2,200,192]{1,2,0:T(8,128)(2,1)}, bf16[2,200,192]{1,2,0:T(8,128)(2,1)}, u32[]{:S(2)}, u32[]{:S(2)}) collective-permute-start(bf16[2,200,192]{1,2,0:T(8,128)(2,1)} %copy.152), channel_id=1, source_target_pairs={{0,1},{1,0},{2,3},{3,2},{4,5},{5,4},{6,7},{7,6},{8,9},{9,8},{10,11... | collective-permute-start | bytes 460808 | tf_op jit(solution)/shard_map/ppermute | solution.py:486
  231.2 22.4 %collective-permute-start = (bf16[2,200,192]{1,2,0:T(8,128)(2,1)}, bf16[2,200,192]{1,2,0:T(8,128)(2,1)}, u32[]{:S(2)}, u32[]{:S(2)}) collective-permute-start(bf16[2,200,192]{1,2,0:T(8,128)(2,1)} %copy.147), channel_id=1, source_target_pairs={{0,1},{1,0},{2,3},{3,2},{4,5},{5,4},{6,7},{7,6},{8,9},{9,8},{10,11... | collective-permute-start | bytes 460808 | tf_op jit(solution)/shard_map/ppermute | solution.py:486
  257.4 41.3 %collective-permute-start.44 = (bf16[2,768,768]{2,1,0:T(8,128)(2,1)}, bf16[2,768,768]{2,1,0:T(8,128)(2,1)}, u32[]{:S(2)}, u32[]{:S(2)}) collective-permute-start(bf16[2,768,768]{2,1,0:T(8,128)(2,1)} %get-tuple-element.141), channel_id=1, source_target_pairs={{0,1},{1,0},{2,3},{3,2},{4,5},{5,4},{6,7},{7,6},{8,9},{9,8},{10,11... | collective-permute-start | bytes 7077896 | tf_op jit(solution)/shard_map/ppermute | solution.py:486
  272.1 29.6 %collective-permute-start.49 = (bf16[2,768,768]{2,1,0:T(8,128)(2,1)}, bf16[2,768,768]{2,1,0:T(8,128)(2,1)}, u32[]{:S(2)}, u32[]{:S(2)}) collective-permute-start(bf16[2,768,768]{2,1,0:T(8,128)(2,1)} %get-tuple-element.143), channel_id=1, source_target_pairs={{0,1},{1,0},{2,3},{3,2},{4,5},{5,4},{6,7},{7,6},{8,9},{9,8},{10,11... | collective-permute-start | bytes 7077896 | tf_op jit(solution)/shard_map/ppermute | solution.py:486
  283.3 22.8 %collective-permute-start.34 = (bf16[2,768,768]{2,1,0:T(8,128)(2,1)}, bf16[2,768,768]{2,1,0:T(8,128)(2,1)}, u32[]{:S(2)}, u32[]{:S(2)}) collective-permute-start(bf16[2,768,768]{2,1,0:T(8,128)(2,1)} %get-tuple-element.137), channel_id=1, source_target_pairs={{0,1},{1,0},{2,3},{3,2},{4,5},{5,4},{6,7},{7,6},{8,9},{9,8},{10,11... | collective-permute-start | bytes 7077896 | tf_op jit(solution)/shard_map/ppermute | solution.py:486
  283.4 24.6 %collective-permute-start.39 = (bf16[2,768,768]{2,1,0:T(8,128)(2,1)}, bf16[2,768,768]{2,1,0:T(8,128)(2,1)}, u32[]{:S(2)}, u32[]{:S(2)}) collective-permute-start(bf16[2,768,768]{2,1,0:T(8,128)(2,1)} %get-tuple-element.139), channel_id=1, source_target_pairs={{0,1},{1,0},{2,3},{3,2},{4,5},{5,4},{6,7},{7,6},{8,9},{9,8},{10,11... | collective-permute-start | bytes 7077896 | tf_op jit(solution)/shard_map/ppermute | solution.py:486
  298.7 25.6 %collective-permute-start.30 = (bf16[2,2,2,96,384]{4,3,2,1,0:T(8,128)(2,1)S(1)}, bf16[2,2,2,96,384]{4,3,2,1,0:T(8,128)(2,1)S(1)}, u32[]{:S(2)}, u32[]{:S(2)}) collective-permute-start(bf16[2,2,2,96,384]{4,3,2,1,0:T(8,128)(2,1)S(1)} %fusion.31), channel_id=1, source_target_pairs={{0,4},{4,0},{8,12},{12,8},{16,20},{20,16},{24,28},{28,24},{1,5},{5... | collective-permute-start | bytes 1769480 | tf_op jit(solution)/shard_map/ppermute | solution.py:486
  301.7 25.1 %collective-permute-start.17 = (bf16[2,2,2,96,384]{4,3,2,1,0:T(8,128)(2,1)S(1)}, bf16[2,2,2,96,384]{4,3,2,1,0:T(8,128)(2,1)S(1)}, u32[]{:S(2)}, u32[]{:S(2)}) collective-permute-start(bf16[2,2,2,96,384]{4,3,2,1,0:T(8,128)(2,1)S(1)} %fusion.28), channel_id=1, source_target_pairs={{0,2},{1,3},{2,0},{3,1},{4,6},{5,7},{6,4},{7,5},{8,10},{9,11},{10,... | collective-permute-start | bytes 1769480 | tf_op jit(solution)/shard_map/ppermute | solution.py:486
  306.1 24.9 %collective-permute-start.26 = (bf16[2,2,2,96,384]{4,3,2,1,0:T(8,128)(2,1)S(1)}, bf16[2,2,2,96,384]{4,3,2,1,0:T(8,128)(2,1)S(1)}, u32[]{:S(2)}, u32[]{:S(2)}) collective-permute-start(bf16[2,2,2,96,384]{4,3,2,1,0:T(8,128)(2,1)S(1)} %fusion.30), channel_id=1, source_target_pairs={{0,2},{1,3},{2,0},{3,1},{4,6},{5,7},{6,4},{7,5},{8,10},{9,11},{10,... | collective-permute-start | bytes 1769480 | tf_op jit(solution)/shard_map/ppermute | solution.py:486
  307.9 113.3 %collective-permute-start.45 = (bf16[2,2,2,96,768]{4,3,2,1,0:T(8,128)(2,1)S(1)}, bf16[2,2,2,96,768]{4,3,2,1,0:T(8,128)(2,1)S(1)}, u32[]{:S(2)}, u32[]{:S(2)}) collective-permute-start(bf16[2,2,2,96,768]{4,3,2,1,0:T(8,128)(2,1)S(1)} %fusion.8), channel_id=1, source_target_pairs={{0,4},{4,0},{8,12},{12,8},{16,20},{20,16},{24,28},{28,24},{1,5},{5... | collective-permute-start | bytes 3538952 | tf_op jit(solution)/shard_map/ppermute | solution.py:486
  311.7 112.9 %collective-permute-start.50 = (bf16[2,2,2,96,768]{4,3,2,1,0:T(8,128)(2,1)S(1)}, bf16[2,2,2,96,768]{4,3,2,1,0:T(8,128)(2,1)S(1)}, u32[]{:S(2)}, u32[]{:S(2)}) collective-permute-start(bf16[2,2,2,96,768]{4,3,2,1,0:T(8,128)(2,1)S(1)} %fusion.9), channel_id=1, source_target_pairs={{0,4},{4,0},{8,12},{12,8},{16,20},{20,16},{24,28},{28,24},{1,5},{5... | collective-permute-start | bytes 3538952 | tf_op jit(solution)/shard_map/ppermute | solution.py:486
  331.0 50.2 %collective-permute-start.18 = (bf16[2,2,96,384]{3,2,1,0:T(8,128)(2,1)S(1)}, bf16[2,2,96,384]{3,2,1,0:T(8,128)(2,1)S(1)}, u32[]{:S(2)}, u32[]{:S(2)}) collective-permute-start(bf16[2,2,96,384]{3,2,1,0:T(8,128)(2,1)S(1)} %fusion.39), channel_id=1, source_target_pairs={{0,4},{4,0},{8,12},{12,8},{16,20},{20,16},{24,28},{28,24},{1,5},{5... | collective-permute-start | bytes 884744 | tf_op jit(solution)/shard_map/ppermute | solution.py:486
  337.3 49.8 %collective-permute-start.27 = (bf16[2,2,96,384]{3,2,1,0:T(8,128)(2,1)S(1)}, bf16[2,2,96,384]{3,2,1,0:T(8,128)(2,1)S(1)}, u32[]{:S(2)}, u32[]{:S(2)}) collective-permute-start(bf16[2,2,96,384]{3,2,1,0:T(8,128)(2,1)S(1)} %fusion.37), channel_id=1, source_target_pairs={{0,4},{4,0},{8,12},{12,8},{16,20},{20,16},{24,28},{28,24},{1,5},{5... | collective-permute-start | bytes 884744 | tf_op jit(solution)/shard_map/ppermute | solution.py:486
  342.9 83.1 %collective-permute-start.35 = (bf16[2,2,2,96,768]{4,3,2,1,0:T(8,128)(2,1)S(1)}, bf16[2,2,2,96,768]{4,3,2,1,0:T(8,128)(2,1)S(1)}, u32[]{:S(2)}, u32[]{:S(2)}) collective-permute-start(bf16[2,2,2,96,768]{4,3,2,1,0:T(8,128)(2,1)S(1)} %fusion.6), channel_id=1, source_target_pairs={{0,2},{1,3},{2,0},{3,1},{4,6},{5,7},{6,4},{7,5},{8,10},{9,11},{10,... | collective-permute-start | bytes 3538952 | tf_op jit(solution)/shard_map/ppermute | solution.py:486
  397.0 34.8 %collective-permute-start.40 = (bf16[2,2,2,96,768]{4,3,2,1,0:T(8,128)(2,1)S(1)}, bf16[2,2,2,96,768]{4,3,2,1,0:T(8,128)(2,1)S(1)}, u32[]{:S(2)}, u32[]{:S(2)}) collective-permute-start(bf16[2,2,2,96,768]{4,3,2,1,0:T(8,128)(2,1)S(1)} %fusion.7), channel_id=1, source_target_pairs={{0,2},{1,3},{2,0},{3,1},{4,6},{5,7},{6,4},{7,5},{8,10},{9,11},{10,... | collective-permute-start | bytes 3538952 | tf_op jit(solution)/shard_map/ppermute | solution.py:486
  425.8 22.6 %collective-permute-start.51 = (bf16[2,2,96,768]{3,2,1,0:T(8,128)(2,1)S(1)}, bf16[2,2,96,768]{3,2,1,0:T(8,128)(2,1)S(1)}, u32[]{:S(2)}, u32[]{:S(2)}) collective-permute-start(bf16[2,2,96,768]{3,2,1,0:T(8,128)(2,1)S(1)} %fusion.10), channel_id=1, source_target_pairs={{0,2},{1,3},{2,0},{3,1},{4,6},{5,7},{6,4},{7,5},{8,10},{9,11},{10,... | collective-permute-start | bytes 1769480 | tf_op jit(solution)/shard_map/ppermute | solution.py:486
  427.3 23.8 %collective-permute-start.36 = (bf16[2,2,96,768]{3,2,1,0:T(8,128)(2,1)S(1)}, bf16[2,2,96,768]{3,2,1,0:T(8,128)(2,1)S(1)}, u32[]{:S(2)}, u32[]{:S(2)}) collective-permute-start(bf16[2,2,96,768]{3,2,1,0:T(8,128)(2,1)S(1)} %fusion.13), channel_id=1, source_target_pairs={{0,4},{4,0},{8,12},{12,8},{16,20},{20,16},{24,28},{28,24},{1,5},{5... | collective-permute-start | bytes 1769480 | tf_op jit(solution)/shard_map/ppermute | solution.py:486
  452.3 20.3 %collective-permute-start.37 = (bf16[2,96,768]{2,1,0:T(8,128)(2,1)S(1)}, bf16[2,96,768]{2,1,0:T(8,128)(2,1)S(1)}, u32[]{:S(2)}, u32[]{:S(2)}) collective-permute-start(bf16[2,96,768]{2,1,0:T(8,128)(2,1)S(1)} %fusion.35), channel_id=1, source_target_pairs={{0,8},{4,12},{8,0},{12,4},{16,24},{20,28},{24,16},{28,20},{1,9},{5... | collective-permute-start | bytes 884744 | tf_op jit(solution)/shard_map/ppermute | solution.py:486
  453.9 22.1 %collective-permute-start.42 = (bf16[2,96,768]{2,1,0:T(8,128)(2,1)S(1)}, bf16[2,96,768]{2,1,0:T(8,128)(2,1)S(1)}, u32[]{:S(2)}, u32[]{:S(2)}) collective-permute-start(bf16[2,96,768]{2,1,0:T(8,128)(2,1)S(1)} %fusion.34), channel_id=1, source_target_pairs={{0,8},{4,12},{8,0},{12,4},{16,24},{20,28},{24,16},{28,20},{1,9},{5... | collective-permute-start | bytes 884744 | tf_op jit(solution)/shard_map/ppermute | solution.py:486
  456.6 21.1 %collective-permute-start.48 = (bf16[96,768]{1,0:T(8,128)(2,1)S(1)}, bf16[96,768]{1,0:T(8,128)(2,1)S(1)}, u32[]{:S(2)}, u32[]{:S(2)}) collective-permute-start(bf16[96,768]{1,0:T(8,128)(2,1)S(1)} %fusion.43), channel_id=1, source_target_pairs={{0,16},{4,20},{8,24},{12,28},{16,0},{20,4},{24,8},{28,12},{1,17},{... | collective-permute-start | bytes 442376 | tf_op jit(solution)/shard_map/ppermute | solution.py:486
  (74 other events, 385.3 us)
